TPU v7x, 128 devices: a whole 4x4x4 slice. The times are simulated.
128 devices in a mesh: dp: 32 (over z, y_hi, x), section: 4 (over y_lo, core).
Axes of the slice: x: 4, y: 4 (y_hi: 2, y_lo: 2; y = y_hi * 2 + y_lo), z: 4, core: 2. Of those that a mesh axis runs over, the one named last changes fastest.
Arguments:
- encoder: bfloat16 [32, 4, 384, 1280], P('dp', 'section'), may hold values from -300 to 300
- destinations: int32 [32, 4, 384, 2], P('dp', 'section'), may hold values from 0 to 31, all different within a row; in each aligned block of 384 rows (0 to 383, 384 to 767, ..., all dimensions but the last counted through in order) at most 48 rows name the same one
- hidden: bfloat16 [32, 4, 256, 1280], P('dp', 'section'), may hold values from -6 to 6
- w_query: bfloat16 [4, 1280, 640], P('section'), may hold values from -0.15625 to 0.15625
- w_key: bfloat16 [4, 1280, 640], P('section'), may hold values from -0.15625 to 0.15625
- w_value: bfloat16 [4, 1280, 640], P('section'), may hold values from -0.15625 to 0.15625
- cotangent: bfloat16 [32, 4, 256, 640], P('dp', 'section'), may hold values from -6 to 6
Outputs:
- attended: bfloat16 [32, 4, 256, 640], P('dp', 'section')
- d_hidden: bfloat16 [32, 4, 256, 1280], P('dp', 'section')
- d_encoder: bfloat16 [32, 4, 384, 1280], P('dp', 'section')
- weight_grads: float32 [4, 1280, 1920], P('section', 'dp')
Inputs may be any that keep to these rules, and one draw needn't show every extreme that they name: `destinations`: each frame names two different readers; in the frames of one device at most 48 name the same reader, and that many do in some device.
All inputs are finite; a program needn't handle non-finite values.
Results may differ from a plain program's by a relative error of at most 0.024.
The roundings to bfloat16 on the way count: a program that leaves them out, or rounds other values in their place, can miss the bound.
Values may be sent and summed in bfloat16 or wider, within the bound.
No kernel may reach another device: no remote copies, remote signals or barrier semaphores. Data moves between devices by JAX's collectives and lax.ppermute only.
A program may use at most 192 MiB of HBM per device.

v0:
```python
import jax
import jax.numpy as jnp
from jax import lax
from jax.sharding import PartitionSpec as P

HEADS = 10
HEAD_DIM = 64


SCALE = 0.125


def passed_along(value, axis, steps):
    count = lax.axis_size(axis)
    pairs = [(source, (source + steps) % count) for source in range(count)]
    return lax.ppermute(value, axis, pairs)


def attend(queries, keys, values, valid, cot):
    dec = queries.shape[0]
    total = keys.shape[0]
    q_heads = queries.reshape(dec, HEADS, HEAD_DIM)
    k_heads = keys.reshape(total, HEADS, HEAD_DIM)
    v_heads = values.reshape(total, HEADS, HEAD_DIM)
    g_heads = cot.reshape(dec, HEADS, HEAD_DIM)
    scores = (
        jnp.einsum("ihd,jhd->hij", q_heads, k_heads, preferred_element_type=jnp.float32) * SCALE
    )
    scores = jnp.where(valid[None, None, :] > 0, scores, -1e30)
    top = jnp.max(scores, axis=-1, keepdims=True)
    expo = jnp.exp(scores - top)
    probs = expo / jnp.sum(expo, axis=-1, keepdims=True)
    probs_b = probs.astype(jnp.bfloat16)
    output = jnp.einsum("hij,jhd->ihd", probs_b, v_heads, preferred_element_type=jnp.float32)
    output = output.reshape(dec, HEADS * HEAD_DIM).astype(jnp.bfloat16)
    dprobs = jnp.einsum("ihd,jhd->hij", g_heads, v_heads, preferred_element_type=jnp.float32)
    dscores = (probs * (dprobs - jnp.sum(probs * dprobs, axis=-1, keepdims=True))).astype(
        jnp.bfloat16
    )
    dq = jnp.einsum("hij,jhd->ihd", dscores, k_heads, preferred_element_type=jnp.float32) * SCALE
    dk = jnp.einsum("hij,ihd->jhd", dscores, q_heads, preferred_element_type=jnp.float32) * SCALE
    dv = jnp.einsum("hij,ihd->jhd", probs_b, g_heads, preferred_element_type=jnp.float32)
    dq = dq.reshape(dec, HEADS * HEAD_DIM).astype(jnp.bfloat16)
    dk = dk.reshape(total, HEADS * HEAD_DIM).astype(jnp.bfloat16)
    dv = dv.reshape(total, HEADS * HEAD_DIM).astype(jnp.bfloat16)
    return (output, dq, dk, dv)


def split_parts(values):
    upper = values.astype(jnp.bfloat16)
    lower = (values - upper.astype(jnp.float32)).astype(jnp.bfloat16)
    return (upper, lower)


def per_device(encoder, destinations, hidden, w_query, w_key, w_value, cotangent):
    own = encoder[0, 0]
    dest = destinations[0, 0]
    wq = w_query[0]
    wk = w_key[0]
    wv = w_value[0]
    rows = own.shape[0]
    width = own.shape[1]
    heads_width = wq.shape[1]
    readers = lax.axis_size("dp")
    capacity = 4 * rows // readers
    targets = jnp.arange(readers, dtype=jnp.int32)
    hit = jnp.any(dest[None, :, :] == targets[:, None, None], axis=-1)
    position = jnp.cumsum(hit.astype(jnp.int32), axis=1) - 1
    slots = jnp.arange(capacity, dtype=jnp.int32)
    table = jnp.logical_and(hit[:, None, :], position[:, None, :] == slots[None, :, None])
    table = table.astype(jnp.bfloat16)
    filled = jnp.sum(table.astype(jnp.float32), axis=-1).astype(jnp.bfloat16)
    w_both = jnp.concatenate([wk, wv], axis=1)
    entering = passed_along(hidden[0, 0], "section", 1)
    queries = jnp.dot(entering, wq, preferred_element_type=jnp.float32).astype(jnp.bfloat16)
    outgoing = jnp.einsum("bcr,rd->bcd", table, own, preferred_element_type=jnp.float32).astype(
        jnp.bfloat16
    )
    arrived, flags = (
        lax.all_to_all(outgoing, "dp", split_axis=0, concat_axis=0, tiled=True),
        lax.all_to_all(filled, "dp", split_axis=0, concat_axis=0, tiled=True),
    )
    memory = jnp.concatenate([own, arrived.reshape(-1, width)], axis=0)
    kv_all = jnp.dot(memory, w_both, preferred_element_type=jnp.float32).astype(jnp.bfloat16)
    keys = kv_all[:, :heads_width]
    values = kv_all[:, heads_width:]
    valid = jnp.concatenate([jnp.ones((rows,), jnp.float32), flags.reshape(-1).astype(jnp.float32)])
    output, dq, dk, dv = attend(queries, keys, values, valid, cotangent[0, 0])
    dentering = jnp.dot(dq, wq.T, preferred_element_type=jnp.float32).astype(jnp.bfloat16)
    d_hidden = passed_along(dentering, "section", -1)
    dkv = jnp.concatenate([dk, dv], axis=1)
    slot_grads = dkv[rows:].reshape(readers, capacity, 2 * heads_width)
    returned = lax.all_to_all(slot_grads, "dp", split_axis=0, concat_axis=0, tiled=True)
    totals = dkv[:rows].astype(jnp.float32)
    totals = totals + jnp.einsum("bcr,bce->re", table, returned, preferred_element_type=jnp.float32)
    upper, lower = split_parts(totals)
    back = (((1,), (1,)), ((), ()))
    d_enc = lax.dot_general(upper, w_both, back, preferred_element_type=jnp.float32)
    d_enc = d_enc + lax.dot_general(lower, w_both, back, preferred_element_type=jnp.float32)
    d_enc = d_enc.astype(jnp.bfloat16)
    contract = (((0,), (0,)), ((), ()))
    part_q = lax.dot_general(entering, dq, contract, preferred_element_type=jnp.float32)
    part_kv = lax.dot_general(memory, dkv, contract, preferred_element_type=jnp.float32)
    grads = lax.psum_scatter(
        jnp.concatenate([part_q, part_kv], axis=1), "dp", scatter_dimension=0, tiled=True
    )
    return (output[None, None], d_hidden[None, None], d_enc[None, None], grads[None])


def solution(mesh):
    return jax.shard_map(
        per_device,
        mesh=mesh,
        in_specs=(
            P("dp", "section", None, None),
            P("dp", "section", None, None),
            P("dp", "section", None, None),
            P("section", None, None),
            P("section", None, None),
            P("section", None, None),
            P("dp", "section", None, None),
        ),
        out_specs=(
            P("dp", "section", None, None),
            P("dp", "section", None, None),
            P("dp", "section", None, None),
            P("section", "dp", None),
        ),
        check_vma=False,
    )
```

profile of v0, /device:TPU:0, one launch (start us, length us, event | category | flops | bytes accessed | tf_op | source)
XLA Modules:
  0.0 619.8 jit_solution(4775037888460500293)
XLA Ops:
  7.2 0.0 copy-start
  7.2 0.8 fusion.47
  8.0 0.9 reduce-window.6
  8.9 0.2 slice_reduce_fusion
  9.2 0.1 copy_bitcast_fusion
  9.3 0.0 copy-start.8
  9.3 0.5 fusion.38
  9.8 0.6 copy.54
  10.4 10.9 %all-to-all-start.1 = ((bf16[32,1,48]{2,1,0:T(2,128)(2,1)}), bf16[32,1,48]{2,1,0:T(2,128)(2,1)S(1)}, u32[]{:S(2)}, u32[]{:S(2)}) async-start(bf16[32,1,48]{2,1,0:T(2,128)(2,1)} %copy.54), calls=%async_computation.1 | async-start | bytes 32768 | tf_op jit(solution)/shard_map/all_to_all | solution.py:81
  21.3 5.4 convolution_convert_fusion.1
  26.6 4.4 all-to-all-done.1
  31.0 0.0 copy-done.8
  31.0 5.7 all-to-all-start
  36.7 0.0 all-reduce.4.cloned.1.call-start
  36.8 0.3 collective-permute-start
  37.0 0.0 copy-done.7
  37.0 0.2 copy.56
  37.2 0.1 reduce.2
  37.3 0.1 convert_element_type.99
  37.4 49.0 %collective-permute-done = bf16[256,1280]{1,0:T(8,128)(2,1)S(1)} collective-permute-done((bf16[256,1280]{1,0:T(8,128)(2,1)}, bf16[256,1280]{1,0:T(8,128)(2,1)S(1)}, u32[]{:S(2)}, u32[]{:S(2)}) %collective-permute-start) | collective-permute-done | bytes 655392 | tf_op jit(solution)/shard_map/ppermute | solution.py:16
  86.4 0.0 copy-done
  86.4 0.7 fusion.35
  87.0 0.2 copy.55
  87.2 1.7 all-to-all-done
  88.9 10.2 %convolution_convert_fusion = bf16[1920,1280]{0,1:T(8,128)(2,1)S(1)} fusion(bf16[1536,1280]{1,0:T(8,128)(2,1)} %bitcast.3, bf16[384,1280]{1,0:T(8,128)(2,1)} %bitcast.110, bf16[1280,640]{1,0:T(8,128)(2,1)} %bitcast.104, bf16[1280,640]{1,0:T(8,128)(2,1)} %bitcast.107), kind=kOutput, calls=%fused_computation.14 | convolution fusion | flops 6310297600 | bytes 13107200 | tf_op jit(solution)/shard_map/dot_general | solution.py:84
  99.1 0.0 copy-done.5
  99.1 2.5 fusion.54
  101.6 11.1 %fusion.55 = (f32[10,256]{1,0:T(8,128)S(1)}, f32[10,256,1920]{2,1,0:T(8,128)}) fusion(pred[1920]{0:T(1024)(128)(4,1)S(1)} %convert_compare_fusion, bf16[256,10,64]{0,2,1:T(8,128)(2,1)S(1)} %bitcast.95, bf16[1920,10,64]{0,2,1:T(8,128)(2,1)} %bitcast.88), kind=kOutput, calls=%fused_computation.73 | convolution fusion | flops 648808320 | bytes 22458240 | tf_op jit(solution)/shard_map/sub | solution.py:31
  112.8 10.0 %fusion.18 = bf16[10,1920,64]{1,2,0:T(8,128)(2,1)} fusion(bf16[256,10,64]{0,2,1:T(8,128)(2,1)S(1)} %bitcast.98, f32[10,256,1920]{2,1,0:T(8,128)} %get-tuple-element.27, f32[10,256]{1,0:T(8,128)S(1)} %get-tuple-element.26), kind=kOutput, calls=%fused_computation.30 | convolution fusion | flops 640204800 | bytes 22456320 | tf_op jit(solution)/shard_map/hij,ihd->jhd/dot_general | solution.py:42
  122.7 0.0 copy-done.4
  122.7 12.4 %fusion.1 = (f32[10,256]{1,0:T(8,128)S(1)}, f32[10,1920,256]{1,2,0:T(8,128)}) fusion(f32[10,256,1920]{2,1,0:T(8,128)} %get-tuple-element.27, f32[10,256]{1,0:T(8,128)S(1)} %get-tuple-element.26, bf16[1920,10,64]{0,2,1:T(8,128)(2,1)S(1)} %bitcast.93, bf16[256,10,64]{0,2,1:T(8,128)(2,1)S(1)} %bitcast.99), kind=kOutput, calls=%fused_computation.3 | convolution fusion | flops 643888640 | bytes 42127360 | tf_op jit(solution)/shard_map/ihd,jhd->hij/dot_general | solution.py:36
  135.1 0.0 copy-done.10
  135.1 13.5 %fusion.3 = bf16[10,256,1920]{2,1,0:T(8,128)(2,1)S(1)} fusion(f32[10,1920,256]{1,2,0:T(8,128)} %get-tuple-element.29, f32[10,256]{1,0:T(8,128)S(1)} %get-tuple-element.28, f32[10,256,1920]{2,1,0:T(8,128)} %get-tuple-element.27, f32[10,256]{1,0:T(8,128)S(1)} %get-tuple-element.26), kind=kLoop, calls=%fused_computation.5 | loop fusion | flops 19660800 | bytes 49172480 | tf_op jit(solution)/shard_map/convert_element_type | solution.py:37
  148.6 0.0 copy-done.1
  148.6 3.8 fusion.31
  152.4 3.0 multiply_convert_fusion
  155.4 4.3 copy.59
  159.8 4.3 copy.58
  164.0 11.1 %fusion.10 = f32[1280,1280]{0,1:T(8,128)S(1)} fusion(bf16[1920,640]{1,0:T(8,128)(2,1)} %copy.59, bf16[1920,640]{1,0:T(8,128)(2,1)} %copy.58, bf16[1536,1280]{1,0:T(8,128)(2,1)} %bitcast.3, bf16[384,1280]{1,0:T(8,128)(2,1)} %bitcast.111), kind=kOutput, calls=%fused_computation.17 | convolution fusion | flops 6311116800 | bytes 16384000 | tf_op jit(solution)/shard_map/dot_general | solution.py:103
  175.2 0.0 copy-done.2
  175.2 0.0 copy-done.6
  175.2 0.6 convolution_bitcast_fusion
  175.8 4.4 pad_maximum_fusion
  180.2 0.0 all-reduce.4.cloned.1.call-update
  180.2 4.4 pad_maximum_fusion.2
  184.6 14.1 %all-to-all-start.2 = ((bf16[32,48,1280]{2,1,0:T(8,128)(2,1)}), bf16[32,48,1280]{2,1,0:T(8,128)(2,1)}, u32[]{:S(2)}, u32[]{:S(2)}) async-start(bf16[32,48,1280]{2,1,0:T(8,128)(2,1)} %bitcast.86), calls=%async_computation.2 | async-start | bytes 7864320 | tf_op jit(solution)/shard_map/all_to_all | solution.py:93
  198.7 0.0 copy-done.14
  198.7 0.6 dynamic-slice
  199.9 0.0 copy-done.3
  200.0 0.7 convolution_convert_fusion.2
  200.7 0.0 copy-start.9
  200.7 0.3 collective-permute-start.1
  201.0 0.0 copy-done.11
  201.1 10.6 %fusion.32 = bf16[10,64,256]{2,1,0:T(8,128)(2,1)S(1)} fusion(bf16[1920,10,64]{0,2,1:T(8,128)(2,1)} %bitcast.92, f32[10,256,1920]{2,1,0:T(8,128)} %get-tuple-element.27, f32[10,256]{1,0:T(8,128)S(1)} %copy-done.11), kind=kOutput, calls=%fused_computation.46 | convolution fusion | flops 639139840 | bytes 22456320 | tf_op jit(solution)/shard_map/hij,jhd->ihd/dot_general | solution.py:34
  211.6 0.9 copy.60
  212.5 69.3 %collective-permute-done.1 = bf16[256,1280]{1,0:T(8,128)(2,1)S(1)} collective-permute-done((bf16[256,1280]{1,0:T(8,128)(2,1)S(1)}, bf16[256,1280]{1,0:T(8,128)(2,1)S(1)}, u32[]{:S(2)}, u32[]{:S(2)}) %collective-permute-start.1) | collective-permute-done | bytes 655392 | tf_op jit(solution)/shard_map/ppermute | solution.py:16
  281.8 0.0 all-to-all-done.2
  281.8 4.4 fusion.21
  286.3 1.5 fusion.44
  287.8 2.5 fusion.23
  290.2 319.0 %all-reduce.4.cloned.1.call-done = f32[1280,1920]{0,1:T(8,128)} async-done(((f32[1280,1920]{0,1:T(8,128)}), f32[1280,1920]{0,1:T(8,128)}) %all-reduce.4.cloned.1.call-update) | async-done | bytes 9830416
  609.2 1.9 dynamic-slice_bitcast_fusion
  611.1 1.0 copy.61
  612.1 0.8 copy.71
  (18 shorter events, 0.1 us)
Async XLA Ops:
  7.2 79.2 %copy-start = (bf16[1,1280,640]{2,1,0:T(8,128)(2,1)S(1)}, bf16[1,1280,640]{2,1,0:T(8,128)(2,1)}, u32[]{:S(2)}) copy-start(bf16[1,1280,640]{2,1,0:T(8,128)(2,1)} %param.10) | copy-start | bytes 4915204
  9.3 21.7 %copy-start.8 = (s32[32,384]{1,0:T(8,128)}, s32[32,384]{1,0:T(8,128)S(1)}, u32[]{:S(2)}) copy-start(s32[32,384]{1,0:T(8,128)S(1)} %copy_bitcast_fusion) | copy-start | bytes 147460
  10.4 20.6 %all-to-all-start.1 = ((bf16[32,1,48]{2,1,0:T(2,128)(2,1)}), bf16[32,1,48]{2,1,0:T(2,128)(2,1)S(1)}, u32[]{:S(2)}, u32[]{:S(2)}) async-start(bf16[32,1,48]{2,1,0:T(2,128)(2,1)} %copy.54), calls=%async_computation.1 | async-start | bytes 32768 | tf_op jit(solution)/shard_map/all_to_all | solution.py:81
  26.6 10.4 %copy-start.7 = (bf16[1,1,256,640]{3,2,1,0:T(8,128)(2,1)S(1)}, bf16[1,1,256,640]{3,2,1,0:T(8,128)(2,1)}, u32[]{:S(2)}) copy-start(bf16[1,1,256,640]{3,2,1,0:T(8,128)(2,1)} %param.13) | copy-start | bytes 983044
  31.0 57.9 %all-to-all-start = ((bf16[32,48,1280]{2,1,0:T(8,128)(2,1)}), bf16[32,48,1280]{2,1,0:T(8,128)(2,1)}, u32[]{:S(2)}, u32[]{:S(2)}) async-start(bf16[32,48,1280]{2,1,0:T(8,128)(2,1)} %convolution_convert_fusion.1), calls=%async_computation | async-start | bytes 7864320 | tf_op jit(solution)/shard_map/all_to_all | solution.py:80
  36.7 572.5 %all-reduce.4.cloned.1.call-start = ((), (), s32[]{:S(2)}) async-start(), calls=%async_computation.3 | async-start | bytes 19660800
  36.8 49.6 %collective-permute-start = (bf16[256,1280]{1,0:T(8,128)(2,1)}, bf16[256,1280]{1,0:T(8,128)(2,1)S(1)}, u32[]{:S(2)}, u32[]{:S(2)}) collective-permute-start(bf16[256,1280]{1,0:T(8,128)(2,1)} %bitcast.8), channel_id=1, source_target_pairs={{0,1},{1,2},{2,3},{3,0},{4,5},{5,6},{6,7},{7,4},{8,9},{9,10},{10,1... | collective-permute-start | bytes 1966088 | tf_op jit(solution)/shard_map/ppermute | solution.py:16
  86.4 12.7 %copy-start.5 = (bf16[256,1280]{1,0:T(8,128)(2,1)}, bf16[256,1280]{1,0:T(8,128)(2,1)S(1)}, u32[]{:S(2)}) copy-start(bf16[256,1280]{1,0:T(8,128)(2,1)S(1)} %collective-permute-done) | copy-start | bytes 1966084
  112.8 22.4 %copy-start.10 = (f32[10,256]{1,0:T(8,128)}, f32[10,256]{1,0:T(8,128)S(1)}, u32[]{:S(2)}) copy-start(f32[10,256]{1,0:T(8,128)S(1)} %get-tuple-element.26) | copy-start | bytes 30724
  112.8 10.0 %copy-start.4 = (bf16[1920,640]{0,1:T(8,128)(2,1)S(1)}, bf16[1920,640]{0,1:T(8,128)(2,1)}, u32[]{:S(2)}) copy-start(bf16[1920,640]{0,1:T(8,128)(2,1)} %get-tuple-element.25) | copy-start | bytes 7372804
  135.1 13.5 %copy-start.1 = (bf16[1920,640]{0,1:T(8,128)(2,1)S(1)}, bf16[1920,640]{0,1:T(8,128)(2,1)}, u32[]{:S(2)}) copy-start(bf16[1920,640]{0,1:T(8,128)(2,1)} %get-tuple-element.24) | copy-start | bytes 7372804
  164.0 11.2 %copy-start.2 = (bf16[10,64,256]{2,1,0:T(8,128)(2,1)S(1)}, bf16[10,64,256]{2,1,0:T(8,128)(2,1)}, u32[]{:S(2)}) copy-start(bf16[10,64,256]{2,1,0:T(8,128)(2,1)} %fusion.31) | copy-start | bytes 983044
  164.0 11.2 %copy-start.6 = (bf16[256,1280]{1,0:T(8,128)(2,1)S(1)}, bf16[256,1280]{1,0:T(8,128)(2,1)}, u32[]{:S(2)}) copy-start(bf16[256,1280]{1,0:T(8,128)(2,1)} %copy-done.5) | copy-start | bytes 1966084
  184.6 14.1 %copy-start.14 = (u32[128]{0:T(128)S(1)}, u32[128]{0:T(128)}, u32[]{:S(2)}) copy-start(u32[128]{0:T(128)} %constant.36) | copy-start | bytes 1540
  184.6 15.3 %copy-start.3 = (bf16[10,64,256]{2,1,0:T(8,128)(2,1)S(1)}, bf16[10,64,256]{2,1,0:T(8,128)(2,1)}, u32[]{:S(2)}) copy-start(bf16[10,64,256]{2,1,0:T(8,128)(2,1)} %fusion.31) | copy-start | bytes 983044
  184.6 16.4 %copy-start.11 = (f32[10,256]{1,0:T(8,128)S(1)}, f32[10,256]{1,0:T(8,128)}, u32[]{:S(2)}) copy-start(f32[10,256]{1,0:T(8,128)} %copy-done.10) | copy-start | bytes 30724
  184.6 97.2 %all-to-all-start.2 = ((bf16[32,48,1280]{2,1,0:T(8,128)(2,1)}), bf16[32,48,1280]{2,1,0:T(8,128)(2,1)}, u32[]{:S(2)}, u32[]{:S(2)}) async-start(bf16[32,48,1280]{2,1,0:T(8,128)(2,1)} %bitcast.86), calls=%async_computation.2 | async-start | bytes 7864320 | tf_op jit(solution)/shard_map/all_to_all | solution.py:93
  200.7 81.1 %copy-start.9 = (s32[32,384]{1,0:T(8,128)S(1)}, s32[32,384]{1,0:T(8,128)}, u32[]{:S(2)}) copy-start(s32[32,384]{1,0:T(8,128)} %copy-done.8) | copy-start | bytes 147460
  200.7 81.1 %collective-permute-start.1 = (bf16[256,1280]{1,0:T(8,128)(2,1)S(1)}, bf16[256,1280]{1,0:T(8,128)(2,1)S(1)}, u32[]{:S(2)}, u32[]{:S(2)}) collective-permute-start(bf16[256,1280]{1,0:T(8,128)(2,1)S(1)} %convolution_convert_fusion.2), channel_id=1, source_target_pairs={{0,3},{1,0},{2,1},{3,2},{4,7},{5,4},{6,5},{7,6},{8,11},{9,8},{10,9... | collective-permute-start | bytes 1966088 | tf_op jit(solution)/shard_map/ppermute | solution.py:16
  281.8 4.4 copy-start.12
  281.8 4.5 copy-start.13
Sparse Core Ops, SparseCore 0:
  180.3 428.8 all-reduce.3
where the time goes:
time: 620 us
  waiting for transfers between devices  443 us (71%)
  matrix products  88 us (14%)
  starting transfers between devices  31.3 us (5%)
  other arithmetic  24.7 us (4%)
  local copies, waits for them, and re-layouts  17.7 us (3%)
  between operations  14.9 us (2%)
    unnamed x2, waiting for transfers between devices  319 us
    ppermute x2, waiting for transfers between devices, passed_along(): return lax.ppermute(value, axis, pairs)  118 us
    all_to_all x1, starting transfers between devices, per_device(): lax.all_to_all(slot_grads, 'dp', split_axis=0, concat_axis=0, tiled=True)  14.1 us
    convert_element_type x1, other arithmetic, attend(): (probs * (dprobs - jnp.sum(probs * dprobs, axis=-1, keepdims=True))).asty...  13.5 us
  transfers between devices with their start and end apart: 6, of which 5 were waited for; matrix products, arithmetic and copies ran while one was open for 5% of the time, Pallas kernels for 0%

commit v1 on v0

--- a/solution.py
+++ b/solution.py
@@ -65,7 +65,10 @@
     capacity = 4 * rows // readers
     targets = jnp.arange(readers, dtype=jnp.int32)
     hit = jnp.any(dest[None, :, :] == targets[:, None, None], axis=-1)
-    position = jnp.cumsum(hit.astype(jnp.int32), axis=1) - 1
+    order = jnp.arange(rows, dtype=jnp.int32)
+    upto = (order[:, None] <= order[None, :]).astype(jnp.bfloat16)
+    position = jnp.dot(hit.astype(jnp.bfloat16), upto, preferred_element_type=jnp.float32)
+    position = position.astype(jnp.int32) - 1
     slots = jnp.arange(capacity, dtype=jnp.int32)
     table = jnp.logical_and(hit[:, None, :], position[:, None, :] == slots[None, :, None])
     table = table.astype(jnp.bfloat16)

time: 620 us -> 620 us (level)
  no operation moved by 1% of the time
where the time goes in v1:
time: 620 us; the launch traced here: 619 us
  waiting for transfers between devices  444 us (72%)
  matrix products  88.2 us (14%)
  starting transfers between devices  31.2 us (5%)
  other arithmetic  23.6 us (4%)
  local copies, waits for them, and re-layouts  17.5 us (3%)
  between operations  14.9 us (2%)
    unnamed x2, waiting for transfers between devices  319 us
    ppermute x2, waiting for transfers between devices, passed_along(): return lax.ppermute(value, axis, pairs)  118 us
    all_to_all x1, starting transfers between devices, per_device(): lax.all_to_all(slot_grads, 'dp', split_axis=0, concat_axis=0, tiled=True)  14 us
    convert_element_type x1, other arithmetic, attend(): (probs * (dprobs - jnp.sum(probs * dprobs, axis=-1, keepdims=True))).asty...  13.5 us
  transfers between devices with their start and end apart: 6, of which 5 were waited for; matrix products, arithmetic and copies ran while one was open for 5% of the time, Pallas kernels for 0%

profile of v1, /device:TPU:0, one launch (start us, length us, event | category | flops | bytes accessed | tf_op | source)
XLA Modules:
  0.0 619.2 jit_solution(1911820166227189018)
XLA Ops:
  7.2 0.0 copy-start
  7.2 0.8 fusion.48
  8.0 0.2 fusion.43
  8.2 0.0 copy-start.8
  8.2 0.5 fusion.38
  8.7 0.6 copy.46
  9.3 10.9 %all-to-all-start.1 = ((bf16[32,1,48]{2,1,0:T(2,128)(2,1)}), bf16[32,1,48]{2,1,0:T(2,128)(2,1)S(1)}, u32[]{:S(2)}, u32[]{:S(2)}) async-start(bf16[32,1,48]{2,1,0:T(2,128)(2,1)} %copy.46), calls=%async_computation.1 | async-start | bytes 32768 | tf_op jit(solution)/shard_map/all_to_all | solution.py:84
  20.2 5.3 convolution_convert_fusion.1
  25.6 4.4 all-to-all-done.1
  29.9 0.0 copy-done.8
  29.9 5.7 all-to-all-start
  35.6 0.0 all-reduce.4.cloned.1.call-start
  35.7 0.3 collective-permute-start
  35.9 0.0 copy-done.7
  35.9 0.2 copy.48
  36.1 0.1 reduce.1
  36.2 0.1 convert_element_type.96
  36.3 49.0 %collective-permute-done = bf16[256,1280]{1,0:T(8,128)(2,1)S(1)} collective-permute-done((bf16[256,1280]{1,0:T(8,128)(2,1)}, bf16[256,1280]{1,0:T(8,128)(2,1)S(1)}, u32[]{:S(2)}, u32[]{:S(2)}) %collective-permute-start) | collective-permute-done | bytes 655392 | tf_op jit(solution)/shard_map/ppermute | solution.py:16
  85.3 0.0 copy-done
  85.3 0.7 fusion.35
  86.0 0.2 copy.47
  86.2 1.7 all-to-all-done
  87.8 10.2 %convolution_convert_fusion = bf16[1920,1280]{0,1:T(8,128)(2,1)S(1)} fusion(bf16[1536,1280]{1,0:T(8,128)(2,1)} %bitcast.3, bf16[384,1280]{1,0:T(8,128)(2,1)} %bitcast.99, bf16[1280,640]{1,0:T(8,128)(2,1)} %bitcast.93, bf16[1280,640]{1,0:T(8,128)(2,1)} %bitcast.96), kind=kOutput, calls=%fused_computation.14 | convolution fusion | flops 6310297600 | bytes 13107200 | tf_op jit(solution)/shard_map/dot_general | solution.py:87
  98.0 0.0 copy-done.5
  98.0 2.6 fusion.55
  100.6 11.2 %fusion.56 = (f32[10,256]{1,0:T(8,128)S(1)}, f32[10,256,1920]{2,1,0:T(8,128)}) fusion(pred[1920]{0:T(1024)(128)(4,1)S(1)} %convert_compare_fusion, bf16[256,10,64]{0,2,1:T(8,128)(2,1)S(1)} %bitcast.85, bf16[1920,10,64]{0,2,1:T(8,128)(2,1)} %bitcast.78), kind=kOutput, calls=%fused_computation.71 | convolution fusion | flops 648808320 | bytes 22458240 | tf_op jit(solution)/shard_map/sub | solution.py:31
  111.7 10.0 %fusion.18 = bf16[10,1920,64]{1,2,0:T(8,128)(2,1)} fusion(bf16[256,10,64]{0,2,1:T(8,128)(2,1)S(1)} %bitcast.88, f32[10,256,1920]{2,1,0:T(8,128)} %get-tuple-element.27, f32[10,256]{1,0:T(8,128)S(1)} %get-tuple-element.26), kind=kOutput, calls=%fused_computation.30 | convolution fusion | flops 640204800 | bytes 22456320 | tf_op jit(solution)/shard_map/hij,ihd->jhd/dot_general | solution.py:42
  121.7 0.0 copy-done.4
  121.7 12.4 %fusion.1 = (f32[10,256]{1,0:T(8,128)S(1)}, f32[10,1920,256]{1,2,0:T(8,128)}) fusion(f32[10,256,1920]{2,1,0:T(8,128)} %get-tuple-element.27, f32[10,256]{1,0:T(8,128)S(1)} %get-tuple-element.26, bf16[1920,10,64]{0,2,1:T(8,128)(2,1)S(1)} %bitcast.83, bf16[256,10,64]{0,2,1:T(8,128)(2,1)S(1)} %bitcast.89), kind=kOutput, calls=%fused_computation.3 | convolution fusion | flops 643888640 | bytes 42127360 | tf_op jit(solution)/shard_map/ihd,jhd->hij/dot_general | solution.py:36
  134.1 0.0 copy-done.10
  134.1 13.5 %fusion.3 = bf16[10,256,1920]{2,1,0:T(8,128)(2,1)S(1)} fusion(f32[10,1920,256]{1,2,0:T(8,128)} %get-tuple-element.29, f32[10,256]{1,0:T(8,128)S(1)} %get-tuple-element.28, f32[10,256,1920]{2,1,0:T(8,128)} %get-tuple-element.27, f32[10,256]{1,0:T(8,128)S(1)} %get-tuple-element.26), kind=kLoop, calls=%fused_computation.5 | loop fusion | flops 19660800 | bytes 49172480 | tf_op jit(solution)/shard_map/convert_element_type | solution.py:37
  147.6 0.0 copy-done.1
  147.6 3.8 fusion.31
  151.4 3.0 multiply_convert_fusion
  154.5 4.3 copy.51
  158.7 4.3 copy.50
  163.0 11.1 %fusion.10 = f32[1280,1280]{0,1:T(8,128)S(1)} fusion(bf16[1920,640]{1,0:T(8,128)(2,1)} %copy.51, bf16[1920,640]{1,0:T(8,128)(2,1)} %copy.50, bf16[1536,1280]{1,0:T(8,128)(2,1)} %bitcast.3, bf16[384,1280]{1,0:T(8,128)(2,1)} %bitcast.100), kind=kOutput, calls=%fused_computation.17 | convolution fusion | flops 6311116800 | bytes 16384000 | tf_op jit(solution)/shard_map/dot_general | solution.py:106
  174.2 0.0 copy-done.2
  174.2 0.0 copy-done.6
  174.2 0.6 convolution_bitcast_fusion
  174.8 4.4 pad_maximum_fusion
  179.1 0.0 all-reduce.4.cloned.1.call-update
  179.2 4.4 pad_maximum_fusion.2
  183.6 14.0 %all-to-all-start.2 = ((bf16[32,48,1280]{2,1,0:T(8,128)(2,1)}), bf16[32,48,1280]{2,1,0:T(8,128)(2,1)}, u32[]{:S(2)}, u32[]{:S(2)}) async-start(bf16[32,48,1280]{2,1,0:T(8,128)(2,1)} %bitcast.76), calls=%async_computation.2 | async-start | bytes 7864320 | tf_op jit(solution)/shard_map/all_to_all | solution.py:96
  197.6 0.0 copy-done.14
  197.6 0.6 dynamic-slice
  198.9 0.0 copy-done.3
  198.9 0.7 convolution_convert_fusion.2
  199.6 0.0 copy-start.9
  199.6 0.3 collective-permute-start.1
  200.0 0.0 copy-done.11
  200.0 10.6 %fusion.32 = bf16[10,64,256]{2,1,0:T(8,128)(2,1)S(1)} fusion(bf16[1920,10,64]{0,2,1:T(8,128)(2,1)} %bitcast.82, f32[10,256,1920]{2,1,0:T(8,128)} %get-tuple-element.27, f32[10,256]{1,0:T(8,128)S(1)} %copy-done.11), kind=kOutput, calls=%fused_computation.46 | convolution fusion | flops 639139840 | bytes 22456320 | tf_op jit(solution)/shard_map/hij,jhd->ihd/dot_general | solution.py:34
  210.5 0.9 copy.52
  211.4 69.3 %collective-permute-done.1 = bf16[256,1280]{1,0:T(8,128)(2,1)S(1)} collective-permute-done((bf16[256,1280]{1,0:T(8,128)(2,1)S(1)}, bf16[256,1280]{1,0:T(8,128)(2,1)S(1)}, u32[]{:S(2)}, u32[]{:S(2)}) %collective-permute-start.1) | collective-permute-done | bytes 655392 | tf_op jit(solution)/shard_map/ppermute | solution.py:16
  280.7 0.0 all-to-all-done.2
  280.7 0.0 copy-done.9
  280.7 4.4 fusion.21
  285.2 0.0 copy-done.12
  285.2 1.5 fusion.45
  286.7 2.5 fusion.23
  289.2 319.5 %all-reduce.4.cloned.1.call-done = f32[1280,1920]{0,1:T(8,128)} async-done(((f32[1280,1920]{0,1:T(8,128)}), f32[1280,1920]{0,1:T(8,128)}) %all-reduce.4.cloned.1.call-update) | async-done | bytes 9830416
  608.6 1.9 dynamic-slice_bitcast_fusion
  610.5 1.0 copy.53
  611.5 0.8 copy.59
  (14 shorter events, 0.0 us)
Async XLA Ops:
  7.2 78.1 %copy-start = (bf16[1,1280,640]{2,1,0:T(8,128)(2,1)S(1)}, bf16[1,1280,640]{2,1,0:T(8,128)(2,1)}, u32[]{:S(2)}) copy-start(bf16[1,1280,640]{2,1,0:T(8,128)(2,1)} %param.10) | copy-start | bytes 4915204
  8.2 21.7 %copy-start.8 = (s32[32,384]{1,0:T(8,128)}, s32[32,384]{1,0:T(8,128)S(1)}, u32[]{:S(2)}) copy-start(s32[32,384]{1,0:T(8,128)S(1)} %fusion.43) | copy-start | bytes 147460
  9.3 20.6 %all-to-all-start.1 = ((bf16[32,1,48]{2,1,0:T(2,128)(2,1)}), bf16[32,1,48]{2,1,0:T(2,128)(2,1)S(1)}, u32[]{:S(2)}, u32[]{:S(2)}) async-start(bf16[32,1,48]{2,1,0:T(2,128)(2,1)} %copy.46), calls=%async_computation.1 | async-start | bytes 32768 | tf_op jit(solution)/shard_map/all_to_all | solution.py:84
  25.6 10.4 %copy-start.7 = (bf16[1,1,256,640]{3,2,1,0:T(8,128)(2,1)S(1)}, bf16[1,1,256,640]{3,2,1,0:T(8,128)(2,1)}, u32[]{:S(2)}) copy-start(bf16[1,1,256,640]{3,2,1,0:T(8,128)(2,1)} %param.13) | copy-start | bytes 983044
  29.9 57.9 %all-to-all-start = ((bf16[32,48,1280]{2,1,0:T(8,128)(2,1)}), bf16[32,48,1280]{2,1,0:T(8,128)(2,1)}, u32[]{:S(2)}, u32[]{:S(2)}) async-start(bf16[32,48,1280]{2,1,0:T(8,128)(2,1)} %convolution_convert_fusion.1), calls=%async_computation | async-start | bytes 7864320 | tf_op jit(solution)/shard_map/all_to_all | solution.py:83
  35.6 573.0 %all-reduce.4.cloned.1.call-start = ((), (), s32[]{:S(2)}) async-start(), calls=%async_computation.3 | async-start | bytes 19660800
  35.7 49.6 %collective-permute-start = (bf16[256,1280]{1,0:T(8,128)(2,1)}, bf16[256,1280]{1,0:T(8,128)(2,1)S(1)}, u32[]{:S(2)}, u32[]{:S(2)}) collective-permute-start(bf16[256,1280]{1,0:T(8,128)(2,1)} %bitcast.8), channel_id=1, source_target_pairs={{0,1},{1,2},{2,3},{3,0},{4,5},{5,6},{6,7},{7,4},{8,9},{9,10},{10,1... | collective-permute-start | bytes 1966088 | tf_op jit(solution)/shard_map/ppermute | solution.py:16
  85.3 12.7 %copy-start.5 = (bf16[256,1280]{1,0:T(8,128)(2,1)}, bf16[256,1280]{1,0:T(8,128)(2,1)S(1)}, u32[]{:S(2)}) copy-start(bf16[256,1280]{1,0:T(8,128)(2,1)S(1)} %collective-permute-done) | copy-start | bytes 1966084
  111.7 22.4 %copy-start.10 = (f32[10,256]{1,0:T(8,128)}, f32[10,256]{1,0:T(8,128)S(1)}, u32[]{:S(2)}) copy-start(f32[10,256]{1,0:T(8,128)S(1)} %get-tuple-element.26) | copy-start | bytes 30724
  111.7 10.0 %copy-start.4 = (bf16[1920,640]{0,1:T(8,128)(2,1)S(1)}, bf16[1920,640]{0,1:T(8,128)(2,1)}, u32[]{:S(2)}) copy-start(bf16[1920,640]{0,1:T(8,128)(2,1)} %get-tuple-element.25) | copy-start | bytes 7372804
  134.1 13.5 %copy-start.1 = (bf16[1920,640]{0,1:T(8,128)(2,1)S(1)}, bf16[1920,640]{0,1:T(8,128)(2,1)}, u32[]{:S(2)}) copy-start(bf16[1920,640]{0,1:T(8,128)(2,1)} %get-tuple-element.24) | copy-start | bytes 7372804
  163.0 11.2 %copy-start.2 = (bf16[10,64,256]{2,1,0:T(8,128)(2,1)S(1)}, bf16[10,64,256]{2,1,0:T(8,128)(2,1)}, u32[]{:S(2)}) copy-start(bf16[10,64,256]{2,1,0:T(8,128)(2,1)} %fusion.31) | copy-start | bytes 983044
  163.0 11.2 %copy-start.6 = (bf16[256,1280]{1,0:T(8,128)(2,1)S(1)}, bf16[256,1280]{1,0:T(8,128)(2,1)}, u32[]{:S(2)}) copy-start(bf16[256,1280]{1,0:T(8,128)(2,1)} %copy-done.5) | copy-start | bytes 1966084
  183.6 14.1 %copy-start.14 = (u32[128]{0:T(128)S(1)}, u32[128]{0:T(128)}, u32[]{:S(2)}) copy-start(u32[128]{0:T(128)} %constant.32) | copy-start | bytes 1540
  183.6 15.3 %copy-start.3 = (bf16[10,64,256]{2,1,0:T(8,128)(2,1)S(1)}, bf16[10,64,256]{2,1,0:T(8,128)(2,1)}, u32[]{:S(2)}) copy-start(bf16[10,64,256]{2,1,0:T(8,128)(2,1)} %fusion.31) | copy-start | bytes 983044
  183.6 16.4 %copy-start.11 = (f32[10,256]{1,0:T(8,128)S(1)}, f32[10,256]{1,0:T(8,128)}, u32[]{:S(2)}) copy-start(f32[10,256]{1,0:T(8,128)} %copy-done.10) | copy-start | bytes 30724
  183.6 97.2 %all-to-all-start.2 = ((bf16[32,48,1280]{2,1,0:T(8,128)(2,1)}), bf16[32,48,1280]{2,1,0:T(8,128)(2,1)}, u32[]{:S(2)}, u32[]{:S(2)}) async-start(bf16[32,48,1280]{2,1,0:T(8,128)(2,1)} %bitcast.76), calls=%async_computation.2 | async-start | bytes 7864320 | tf_op jit(solution)/shard_map/all_to_all | solution.py:96
  199.6 81.1 %copy-start.9 = (s32[32,384]{1,0:T(8,128)S(1)}, s32[32,384]{1,0:T(8,128)}, u32[]{:S(2)}) copy-start(s32[32,384]{1,0:T(8,128)} %copy-done.8) | copy-start | bytes 147460
  199.6 81.1 %collective-permute-start.1 = (bf16[256,1280]{1,0:T(8,128)(2,1)S(1)}, bf16[256,1280]{1,0:T(8,128)(2,1)S(1)}, u32[]{:S(2)}, u32[]{:S(2)}) collective-permute-start(bf16[256,1280]{1,0:T(8,128)(2,1)S(1)} %convolution_convert_fusion.2), channel_id=1, source_target_pairs={{0,3},{1,0},{2,1},{3,2},{4,7},{5,4},{6,5},{7,6},{8,11},{9,8},{10,9... | collective-permute-start | bytes 1966088 | tf_op jit(solution)/shard_map/ppermute | solution.py:16
  280.7 4.4 copy-start.12
  280.7 4.5 copy-start.13
Sparse Core Ops, SparseCore 0:
  179.3 429.3 all-reduce.3

commit v2 on v0

v2 whole, which is shorter than its diff:
```python
import functools

import jax
import jax.numpy as jnp
from jax import lax
from jax.experimental import pallas as pl
from jax.experimental.pallas import tpu as pltpu
from jax.sharding import PartitionSpec as P

PAIR = 128
CHUNKS = (2, 3)
SLOTS, ROWS, TWICE = 48, 40, 24
SENT = SLOTS + ROWS + TWICE
SCALE = 0.125
F32 = jnp.float32
BF16 = jnp.bfloat16
VMEM_LIMIT = 60 * 1024 * 1024

NT = (((1,), (1,)), ((), ()))
NN = (((1,), (0,)), ((), ()))


def mm(a, b, dims=NN):
    return lax.dot_general(a, b, dims, preferred_element_type=F32)


def params(**kw):
    return pltpu.CompilerParams(vmem_limit_bytes=VMEM_LIMIT, **kw)


def cost(flops, bytes_accessed, transcendentals=0):
    return pl.CostEstimate(
        flops=flops, bytes_accessed=bytes_accessed, transcendentals=transcendentals
    )


def passed_along(value, axis, steps):
    count = lax.axis_size(axis)
    pairs = [(source, (source + steps) % count) for source in range(count)]
    return lax.ppermute(value, axis, pairs)


def exchanged(value):
    return lax.all_to_all(value, "dp", split_axis=0, concat_axis=0, tiled=True)


def slots_along_lanes(dc, dr, capacity):
    rows = dr.shape[1]
    shape = (rows, rows)
    before = lax.broadcasted_iota(jnp.int32, shape, 0) < lax.broadcasted_iota(
        jnp.int32, shape, 1
    )
    found = []
    for which in range(2):
        mine = dr[which : which + 1, :]
        same = jnp.logical_or(dc[:, 0:1] == mine, dc[:, 1:2] == mine)
        earlier = jnp.where(jnp.logical_and(same, before), 1.0, 0.0)
        place = jnp.sum(earlier, axis=0, keepdims=True).astype(jnp.int32)
        found.append(mine * capacity + place)
    return found


def slots_along_sublanes(dc, dr, capacity):
    rows = dr.shape[1]
    shape = (rows, rows)
    before = lax.broadcasted_iota(jnp.int32, shape, 1) < lax.broadcasted_iota(
        jnp.int32, shape, 0
    )
    found = []
    for which in range(2):
        mine = dc[:, which : which + 1]
        same = jnp.logical_or(dr[0:1, :] == mine, dr[1:2, :] == mine)
        earlier = jnp.where(jnp.logical_and(same, before), 1.0, 0.0)
        place = jnp.sum(earlier, axis=1, keepdims=True).astype(jnp.int32)
        found.append(mine * capacity + place)
    return found


def dispatch_kernel(capacity, dc_ref, dr_ref, own_ref, out_ref):
    rows = own_ref.shape[0]
    both = jnp.concatenate([own_ref[...], jnp.ones((rows, PAIR), BF16)], axis=1)
    slot_a, slot_b = slots_along_lanes(dc_ref[...], dr_ref[...], capacity)
    for block in range(out_ref.shape[0] // rows):
        at = lax.broadcasted_iota(jnp.int32, (rows, rows), 0) + block * rows
        table = jnp.logical_or(at == slot_a, at == slot_b)
        table = jnp.where(table, 1.0, 0.0).astype(BF16)
        out_ref[pl.ds(block * rows, rows), :] = mm(table, both).astype(BF16)


def dispatch(capacity, readers, dc, dr, own):
    rows, width = own.shape
    slots = readers * capacity
    return pl.pallas_call(
        functools.partial(dispatch_kernel, capacity),
        out_shape=jax.ShapeDtypeStruct((slots, width + PAIR), BF16),
        compiler_params=params(),
        cost_estimate=cost(2 * rows * width * slots, 2 * width * (rows + slots)),
        name="dispatch",
    )(dc, dr, own)


def attend_kernel(held, *refs):
    q_ref, g_ref, own_ref, got_ref, wk_ref, wv_ref, entering_ref = refs[:7]
    o_ref, dq_ref, down_ref, sent_ref = refs[7 + held : 11 + held]
    kv_ref, s_ref, dp_ref, mem_t_ref, entering_t_ref = refs[11 + held :]
    readers = sent_ref.shape[0]
    dec = q_ref.shape[0]
    tile, width = own_ref.shape
    tiles = 1 + got_ref.shape[0] // tile
    lane = lax.broadcasted_iota(jnp.int32, (dec, PAIR), 1)
    q = q_ref[...] * jnp.asarray(SCALE, BF16)
    g = g_ref[...]
    zero = jnp.zeros_like(q)
    head = [lane < PAIR // 2, lane >= PAIR // 2]
    q_both = jnp.concatenate([jnp.where(head[h], q, zero) for h in range(2)], axis=0)
    g_both = jnp.concatenate([jnp.where(head[h], g, zero) for h in range(2)], axis=0)
    weights = jnp.concatenate([wk_ref[...], wv_ref[...]], axis=1)

    def frames(t):
        if t == 0:
            return own_ref[...]
        return got_ref[pl.ds((t - 1) * tile, tile), :width]

    @pl.when(pl.program_id(0) == 0)
    def _():
        for t in range(tiles):
            mem_t_ref[:, t * tile : (t + 1) * tile] = frames(t).T
        entering_t_ref[...] = entering_ref[...].T

    tops = []
    for t in range(tiles):
        at = pl.ds(t * tile, tile)
        kv = mm(frames(t), weights).astype(BF16)
        kv_ref[at, :] = kv
        s = mm(kv[:, :PAIR], q_both, NT)
        if t > 0:
            flag = got_ref[pl.ds((t - 1) * tile, tile), width : width + PAIR]
            s = s + (flag.astype(F32)[:, 0:1] - 1.0) * 1e30
        s_ref[at, :] = s
        tops.append(jnp.max(s, axis=0, keepdims=True))
    top = functools.reduce(jnp.maximum, tops)
    total = jnp.zeros_like(top)
    inner = jnp.zeros_like(top)
    for t in range(tiles):
        at = pl.ds(t * tile, tile)
        e = jnp.exp(s_ref[at, :] - top)
        s_ref[at, :] = e
        total = total + jnp.sum(e, axis=0, keepdims=True)
        dp = mm(kv_ref[at, PAIR:], g_both, NT)
        dp_ref[at, :] = dp
        inner = inner + jnp.sum(e * dp, axis=0, keepdims=True)
    inverse = 1.0 / total
    inner = inner * inverse
    half = PAIR // 2
    out_t = [jnp.zeros((half, dec), F32) for _ in range(2)]
    dq_t = [jnp.zeros((half, dec), F32) for _ in range(2)]
    for t in range(tiles):
        at = pl.ds(t * tile, tile)
        kv_t = kv_ref[at, :].T
        p = s_ref[at, :] * inverse
        pb = p.astype(BF16)
        ds = (p * (dp_ref[at, :] - inner)).astype(BF16)
        for h in range(2):
            cols = slice(h * dec, (h + 1) * dec)
            dq_t[h] = dq_t[h] + mm(kv_t[h * half : (h + 1) * half], ds[:, cols])
            out_t[h] = out_t[h] + mm(kv_t[PAIR + h * half : PAIR + (h + 1) * half], pb[:, cols])
        dk = mm(ds, q_both)
        dv = mm(pb, g_both)
        dkv = jnp.concatenate([dk, dv], axis=1).astype(BF16)
        kv_ref[at, :] = dkv
        if t == 0:
            down_ref[...] = dkv
        else:
            count = tile // SLOTS
            dkv = dkv.reshape(count, SLOTS, 2 * PAIR)
            sent_ref[pl.ds((t - 1) * count, count), :SLOTS, :] = dkv
    o_ref[...] = jnp.concatenate(out_t, axis=0).T.astype(BF16)
    dq = (jnp.concatenate(dq_t, axis=0) * SCALE).T.astype(BF16)
    dq_ref[...] = dq
    grad = mm(mem_t_ref[...], kv_ref[...]).reshape(readers, ROWS, 2 * PAIR)
    sent_ref[:, SLOTS : SLOTS + ROWS, :] = grad.astype(BF16)
    grad = mm(entering_t_ref[...], dq).reshape(readers, ROWS, PAIR)
    grad = jnp.concatenate([grad[:, :TWICE], grad[:, ROWS - TWICE :]], axis=2)
    sent_ref[:, SLOTS + ROWS :, :] = grad.astype(BF16)


def attend(first, pairs, readers, queries, cot, own, got, wk, wv, entering, filled):
    dec, heads = queries.shape
    rows, width = own.shape
    slots = got.shape[0]
    total = rows + slots
    pair_at = lambda p: (0, first + p)
    whole = lambda p: (0, 0)
    return pl.pallas_call(
        functools.partial(attend_kernel, len(filled)),
        grid=(pairs,),
        in_specs=[
            pl.BlockSpec((dec, PAIR), pair_at),
            pl.BlockSpec((dec, PAIR), pair_at),
            pl.BlockSpec((rows, width), whole),
            pl.BlockSpec((slots, width + PAIR), whole),
            pl.BlockSpec((width, PAIR), pair_at),
            pl.BlockSpec((width, PAIR), pair_at),
            pl.BlockSpec((dec, width), whole),
        ]
        + [pl.BlockSpec(memory_space=pl.ANY)] * len(filled),
        out_specs=[
            pl.BlockSpec((dec, PAIR), pair_at),
            pl.BlockSpec((dec, PAIR), pair_at),
            pl.BlockSpec((rows, 2 * PAIR), pair_at),
            pl.BlockSpec((readers, SENT, 2 * PAIR), lambda p: (0, 0, p)),
        ],
        out_shape=(
            jax.ShapeDtypeStruct((dec, heads), BF16),
            jax.ShapeDtypeStruct((dec, heads), BF16),
            jax.ShapeDtypeStruct((rows, 2 * heads), BF16),
            jax.ShapeDtypeStruct((readers, SENT, 2 * PAIR * pairs), BF16),
        ),
        scratch_shapes=[
            pltpu.VMEM((total, 2 * PAIR), BF16),
            pltpu.VMEM((total, 2 * dec), F32),
            pltpu.VMEM((total, 2 * dec), F32),
            pltpu.VMEM((width, total), BF16),
            pltpu.VMEM((width, dec), BF16),
        ],
        input_output_aliases={7 + i: i for i in range(len(filled))},
        compiler_params=params(dimension_semantics=("arbitrary",)),
        cost_estimate=cost(
            pairs * (12 * dec * total * PAIR * 4 + 8 * width * total * PAIR),
            2 * total * width + pairs * 12 * total * PAIR,
            pairs * 2 * dec * total,
        ),
        name=f"attend_{first}",
    )(queries, cot, own, got, wk, wv, entering, *filled)


def query_kernel(dq_ref, wq_ref, dent_ref):
    dent_ref[...] = mm(dq_ref[...], wq_ref[...], NT).astype(BF16)


def query_side(dq, wq):
    dec = dq.shape[0]
    width, heads = wq.shape
    return pl.pallas_call(
        query_kernel,
        out_shape=jax.ShapeDtypeStruct((dec, width), BF16),
        compiler_params=params(),
        cost_estimate=cost(2 * dec * width * heads, 2 * width * (dec + heads)),
        name="query_side",
    )(dq, wq)


def combine_kernel(first, capacity, last, dc_ref, dr_ref, down_ref, back_ref, wk_ref, wv_ref, *refs):
    held, out_ref = refs[:-1], refs[-1]
    rows = down_ref.shape[0]
    lanes = back_ref.shape[2]
    slot_a, slot_b = slots_along_sublanes(dc_ref[...], dr_ref[...], capacity)
    tot = down_ref[:, 2 * first * PAIR : 2 * first * PAIR + lanes].astype(F32)
    count = rows // SLOTS
    for block in range(back_ref.shape[0] // count):
        at = lax.broadcasted_iota(jnp.int32, (rows, rows), 1) + block * rows
        table = jnp.logical_or(at == slot_a, at == slot_b)
        table = jnp.where(table, 1.0, 0.0).astype(BF16)
        part = back_ref[pl.ds(block * count, count), :, :].reshape(rows, lanes)
        tot = tot + mm(table, part)
    tot = tot.astype(BF16)
    pieces = [tot[:, c * PAIR : (c + 1) * PAIR] for c in range(lanes // PAIR)]
    cut = slice(first * PAIR, first * PAIR + lanes // 2)
    out = mm(jnp.concatenate(pieces[0::2], axis=1), wk_ref[:, cut], NT)
    out = out + mm(jnp.concatenate(pieces[1::2], axis=1), wv_ref[:, cut], NT)
    for r in held:
        out = out + r[...]
    out_ref[...] = out.astype(out_ref.dtype)


def combine(first, last, capacity, dc, dr, down, back, wk, wv, held):
    rows = down.shape[0]
    width, heads = wk.shape
    readers, _, lanes = back.shape
    whole = lambda i: (0, 0)
    full = lambda a: pl.BlockSpec(a.shape, whole)
    return pl.pallas_call(
        functools.partial(combine_kernel, first, capacity, last),
        grid=(1,),
        in_specs=[
            full(dc),
            full(dr),
            full(down),
            pl.BlockSpec((readers, SLOTS, lanes), lambda i: (0, 0, 0)),
            full(wk),
            full(wv),
        ]
        + [full(h) for h in held],
        out_specs=pl.BlockSpec((rows, width), whole),
        out_shape=jax.ShapeDtypeStruct((rows, width), BF16 if last else F32),
        compiler_params=params(),
        cost_estimate=cost(
            2 * rows * lanes * (width + readers * SLOTS),
            2 * (rows * width + width * lanes + readers * SLOTS * lanes),
        ),
        name=f"combine_{first}",
    )(dc, dr, down, back, wk, wv, *held)


def sum_kernel(back_ref, out_ref):
    sums = [back_ref[a].astype(F32) for a in range(4)]
    for a in range(4, back_ref.shape[0]):
        sums[a % 4] = sums[a % 4] + back_ref[a].astype(F32)
    out_ref[...] = (sums[0] + sums[1]) + (sums[2] + sums[3])


def summed(first, back):
    readers, rows, lanes = back.shape
    step = 16
    return pl.pallas_call(
        sum_kernel,
        grid=((rows - SLOTS) // step,),
        in_specs=[pl.BlockSpec((readers, step, lanes), lambda i: (0, SLOTS // step + i, 0))],
        out_specs=pl.BlockSpec((step, lanes), lambda i: (i, 0)),
        out_shape=jax.ShapeDtypeStruct((rows - SLOTS, lanes), F32),
        compiler_params=params(),
        cost_estimate=cost(readers * rows * lanes, 2 * readers * rows * lanes),
        name=f"summed_{first}",
    )(back)


def gather_kernel(*refs):
    parts, out_ref = refs[:-1], refs[-1]
    heads = out_ref.shape[1] // 3
    both = jnp.concatenate([r[...] for r in parts], axis=1)
    pieces = [both[:, c * PAIR : (c + 1) * PAIR] for c in range(2 * heads // PAIR)]
    upper = jnp.concatenate(pieces[0::2], axis=1)
    lower = jnp.concatenate(pieces[1::2], axis=1)
    out_ref[:TWICE, :heads] = upper[ROWS:]
    out_ref[TWICE:, :heads] = lower[2 * TWICE :]
    out_ref[:, heads : 2 * heads] = upper[:ROWS]
    out_ref[:, 2 * heads :] = lower[:ROWS]


def gathered(heads, parts):
    return pl.pallas_call(
        gather_kernel,
        out_shape=jax.ShapeDtypeStruct((ROWS, 3 * heads), F32),
        compiler_params=params(),
        cost_estimate=cost(0, 24 * ROWS * heads),
        name="gathered",
    )(*parts)


def per_device(encoder, destinations, hidden, w_query, w_key, w_value, cotangent):
    own = encoder[0, 0]
    dest = destinations[0, 0]
    wq, wk, wv = w_query[0], w_key[0], w_value[0]
    cot = cotangent[0, 0]
    rows, width = own.shape
    heads = wq.shape[1]
    readers = lax.axis_size("dp")
    capacity = 4 * rows // readers
    dest_rows = dest.T

    slots = readers * capacity

    slots = readers * capacity

    entering = passed_along(hidden[0, 0], "section", 1)
    out = dispatch(capacity, readers, dest, dest_rows, own)
    out, entering = lax.optimization_barrier((out, entering))
    queries = jnp.dot(entering, wq, preferred_element_type=F32).astype(BF16)
    got = exchanged(out.reshape(readers, capacity, -1)).reshape(slots, -1)

    filled, backs, firsts, first = (), [], [], 0
    for pairs in CHUNKS:
        *filled, sent = attend(
            first, pairs, readers, queries, cot, own, got, wk, wv, entering, filled
        )
        backs.append(exchanged(sent))
        firsts.append(first)
        first += pairs
    attended, dq, down = filled
    dentering = query_side(dq, wq)
    held, grads = [], []
    for c, first in enumerate(firsts):
        last = c == len(firsts) - 1
        if held:
            backs[c], held, grads, down, dentering = lax.optimization_barrier(
                (backs[c], held, grads, down, dentering)
            )
        if last:
            d_hidden = passed_along(dentering, "section", -1)
        held = [
            combine(first, last, capacity, dest, dest_rows, down, backs[c], wk, wv, held)
        ]
        grads.append(summed(first, backs[c]))
    d_enc = held[0]
    grads = gathered(heads, grads)
    return (attended[None, None], d_hidden[None, None], d_enc[None, None], grads[None])


def solution(mesh):
    return jax.shard_map(
        per_device,
        mesh=mesh,
        in_specs=(
            P("dp", "section", None, None),
            P("dp", "section", None, None),
            P("dp", "section", None, None),
            P("section", None, None),
            P("section", None, None),
            P("section", None, None),
            P("dp", "section", None, None),
        ),
        out_specs=(
            P("dp", "section", None, None),
            P("dp", "section", None, None),
            P("dp", "section", None, None),
            P("section", "dp", None),
        ),
        check_vma=False,
    )
```

time: 620 us -> 263 us (0.42)
  the two profiles are of different devices: /device:TPU:0 before, /device:TPU:11 now
where the time goes in v2:
time: 263 us
  waiting for transfers between devices  142 us (54%)
  Pallas kernels  89.4 us (34%)
  starting transfers between devices  27.1 us (10%)
    all_to_all x3, waiting for transfers between devices, exchanged(): return lax.all_to_all(value, 'dp', split_axis=0, concat_axis=0, tiled=True)  141 us
    pallas_call x2, Pallas kernels, attend(): pl.pallas_call(functools.partial(attend_kernel, len(filled)), grid=(pairs...  55.7 us
    all_to_all x3, starting transfers between devices, exchanged(): return lax.all_to_all(value, 'dp', split_axis=0, concat_axis=0, tiled=True)  24.6 us
    pallas_call x2, Pallas kernels, combine(): pl.pallas_call(functools.partial(combine_kernel, first, capacity, last),...  15.6 us
    pallas_call x2, Pallas kernels, summed(): pl.pallas_call(sum_kernel, grid=((rows - SLOTS) // step,), in_specs=[pl.B...  7.29 us
    pallas_call x1, Pallas kernels, dispatch(): pl.pallas_call(functools.partial(dispatch_kernel, capacity), out_shape=ja...  6.03 us
  transfers between devices with their start and end apart: 5, of which 4 were waited for; matrix products, arithmetic and copies ran while one was open for 1% of the time, Pallas kernels for 25%

profile of v2, /device:TPU:11, one launch (start us, length us, event | category | flops | bytes accessed | tf_op | source)
XLA Modules:
  0.0 262.7 jit_solution(6147185120868022041)
XLA Ops:
  0.6 0.8 collective-permute-start
  1.4 1.5 copy.14.dc_ref
  2.9 6.0 %dispatch.1 = bf16[1536,1408]{1,0:T(8,128)(2,1)} custom-call(s32[384,2]{1,0:T(8,128)} %copy.14.dc_ref, s32[2,384]{1,0:T(2,128)} %bitcast.32, bf16[384,1280]{1,0:T(8,128)(2,1)} %bitcast.35), custom_call_target="tpu_custom_call" | custom-call | flops 1509949440 | bytes 4915200 | tf_op jit(solution)/shard_map/dispatch/pallas_call | solution.py:93
  9.0 0.3 collective-permute-done.refs_6_
  9.3 0.0 copy-start.2
  9.3 0.0 copy-start
  9.3 10.1 %all-to-all-start = ((bf16[32,48,1408]{2,1,0:T(8,128)(2,1)}), bf16[32,48,1408]{2,1,0:T(8,128)(2,1)}, u32[]{:S(2)}, u32[]{:S(2)}) async-start(bf16[32,48,1408]{2,1,0:T(8,128)(2,1)} %bitcast.26), calls=%async_computation | async-start | bytes 8650752 | tf_op jit(solution)/shard_map/all_to_all | solution.py:44
  19.4 0.0 copy-done.2
  19.4 0.0 copy-done
  19.4 1.4 convolution_convert_fusion.refs_0_
  20.8 59.9 %all-to-all-done = bf16[32,48,1408]{2,1,0:T(8,128)(2,1)} async-done(((bf16[32,48,1408]{2,1,0:T(8,128)(2,1)}), bf16[32,48,1408]{2,1,0:T(8,128)(2,1)}, u32[]{:S(2)}, u32[]{:S(2)}) %all-to-all-start) | async-done | bytes 4325408 | tf_op jit(solution)/shard_map/all_to_all | solution.py:44
  80.7 23.4 %attend_0.1 = (bf16[256,640]{1,0:T(8,128)(2,1)}, bf16[256,640]{1,0:T(8,128)(2,1)}, bf16[384,1280]{1,0:T(8,128)(2,1)}, bf16[32,112,512]{2,1,0:T(8,128)(2,1)}) custom-call(bf16[256,640]{1,0:T(8,128)(2,1)} %convolution_convert_fusion.refs_0_, bf16[256,640]{1,0:T(8,128)(2,1)} %bitcast.39, bf16[384,1280]{1,0:T(8,128)(2,1)} %bitcast.36, ...), custom_call_target="tpu_custom_call" | custom-call | flops 11072962560 | bytes 10813440 | tf_op jit(solution)/shard_map/attend_0/pallas_call | solution.py:194
  104.1 5.3 %all-to-all-start.2 = ((bf16[32,112,512]{2,1,0:T(8,128)(2,1)}), bf16[32,112,512]{2,1,0:T(8,128)(2,1)}, u32[]{:S(2)}, u32[]{:S(2)}) async-start(bf16[32,112,512]{2,1,0:T(8,128)(2,1)} %get-tuple-element.27), calls=%async_computation.2 | async-start | bytes 7340032 | tf_op jit(solution)/shard_map/all_to_all | solution.py:44
  109.4 32.3 %attend_2.1 = (bf16[256,640]{1,0:T(8,128)(2,1)}, bf16[256,640]{1,0:T(8,128)(2,1)}, bf16[384,1280]{1,0:T(8,128)(2,1)}, bf16[32,112,768]{2,1,0:T(8,128)(2,1)}) custom-call(bf16[256,640]{1,0:T(8,128)(2,1)} %convolution_convert_fusion.refs_0_, bf16[256,640]{1,0:T(8,128)(2,1)} %bitcast.40, ...), custom_call_target="tpu_custom_call", output_to_operand_aliasing={{0}: (7, {}), {1}: (8, {}), {2}: (9, {})} | custom-call | flops 16609443840 | bytes 13762560 | tf_op jit(solution)/shard_map/attend_2/pallas_call | solution.py:194
  141.7 14.6 %all-to-all-done.2.back_ref = bf16[32,112,512]{2,1,0:T(8,128)(2,1)} async-done(((bf16[32,112,512]{2,1,0:T(8,128)(2,1)}), bf16[32,112,512]{2,1,0:T(8,128)(2,1)}, u32[]{:S(2)}, u32[]{:S(2)}) %all-to-all-start.2) | async-done | bytes 3670048 | tf_op jit(solution)/shard_map/all_to_all | solution.py:44
  156.3 9.1 %all-to-all-start.1 = ((bf16[32,112,768]{2,1,0:T(8,128)(2,1)}), bf16[32,112,768]{2,1,0:T(8,128)(2,1)}, u32[]{:S(2)}, u32[]{:S(2)}) async-start(bf16[32,112,768]{2,1,0:T(8,128)(2,1)} %get-tuple-element.25), calls=%async_computation.1 | async-start | bytes 11010048 | tf_op jit(solution)/shard_map/all_to_all | solution.py:44
  165.5 3.1 %query_side.1 = bf16[256,1280]{1,0:T(8,128)(2,1)} custom-call(bf16[256,640]{1,0:T(8,128)(2,1)} %get-tuple-element.28.dq_ref, bf16[1280,640]{1,0:T(8,128)(2,1)} %bitcast.27), custom_call_target="tpu_custom_call" | custom-call | flops 419430400 | bytes 2293760 | tf_op jit(solution)/shard_map/query_side/pallas_call | solution.py:244
  168.6 3.5 %summed_0.1.refs_0_ = f32[64,512]{1,0:T(8,128)} custom-call(bf16[32,112,512]{2,1,0:T(8,128)(2,1)} %all-to-all-done.2.back_ref), custom_call_target="tpu_custom_call" | custom-call | flops 1835008 | bytes 3670016 | tf_op jit(solution)/shard_map/summed_0/pallas_call | solution.py:315
  172.1 0.0 copy-start.1
  172.1 6.8 %combine_0.1.refs_0_ = f32[384,1280]{1,0:T(8,128)} custom-call(s32[384,2]{1,0:T(8,128)} %copy.14.dc_ref, s32[2,384]{1,0:T(2,128)} %bitcast.33, bf16[384,1280]{1,0:T(8,128)(2,1)} %get-tuple-element.30.down_ref, bf16[32,112,512]{2,1,0:T(8,128)(2,1)} %all-to-all-done.2.back_ref, bf16[1280,640]{1,0:T(8,128)(2,1)} %bitcast.20, bf16[1280,640]{1,0:T(8,128)(2,1)} %bitcast.24), custom_call_target="tpu_custom_call" | custom-call | flops 1107296256 | bytes 3866624 | tf_op jit(solution)/shard_map/combine_0/pallas_call | solution.py:282
  178.9 66.9 %all-to-all-done.1.back_ref = bf16[32,112,768]{2,1,0:T(8,128)(2,1)} async-done(((bf16[32,112,768]{2,1,0:T(8,128)(2,1)}), bf16[32,112,768]{2,1,0:T(8,128)(2,1)}, u32[]{:S(2)}, u32[]{:S(2)}) %all-to-all-start.1) | async-done | bytes 5505056 | tf_op jit(solution)/shard_map/all_to_all | solution.py:44
  245.8 0.0 copy-done.1
  245.8 1.8 collective-permute-start.1
  247.5 3.8 %summed_2.1.refs_1_ = f32[64,768]{1,0:T(8,128)} custom-call(bf16[32,112,768]{2,1,0:T(8,128)(2,1)} %all-to-all-done.1.back_ref), custom_call_target="tpu_custom_call" | custom-call | flops 2752512 | bytes 5505024 | tf_op jit(solution)/shard_map/summed_2/pallas_call | solution.py:315
  251.3 1.7 gathered.1
  253.1 8.8 %combine_2.1 = bf16[384,1280]{1,0:T(8,128)(2,1)} custom-call(s32[384,2]{1,0:T(8,128)} %copy.14.dc_ref, s32[2,384]{1,0:T(2,128)} %bitcast.34, bf16[384,1280]{1,0:T(8,128)(2,1)} %get-tuple-element.30.down_ref, bf16[32,112,768]{2,1,0:T(8,128)(2,1)} %all-to-all-done.1.back_ref, bf16[1280,640]{1,0:T(8,128)(2,1)} %bitcast.21, bf16[1280,640]{1,0:T(8,128)(2,1)} %bitcast.25, ...), custom_call_target="tpu_custom_call" | custom-call | flops 1660944384 | bytes 5308416 | tf_op jit(solution)/shard_map/combine_2/pallas_call | solution.py:282
  261.9 0.0 collective-permute-done.1
  261.9 0.8 copy.21
Async XLA Ops:
  0.6 8.6 %collective-permute-start = (bf16[256,1280]{1,0:T(8,128)(2,1)}, bf16[256,1280]{1,0:T(8,128)(2,1)S(1)}, u32[]{:S(2)}, u32[]{:S(2)}) collective-permute-start(bf16[256,1280]{1,0:T(8,128)(2,1)} %bitcast.38), channel_id=1, source_target_pairs={{0,1},{1,2},{2,3},{3,0},{4,5},{5,6},{6,7},{7,4},{8,9},{9,10},{10,1... | collective-permute-start | bytes 1966088 | tf_op jit(solution)/shard_map/ppermute | solution.py:40
  9.3 10.1 %copy-start.2 = (bf16[256,1280]{1,0:T(8,128)(2,1)}, bf16[256,1280]{1,0:T(8,128)(2,1)S(1)}, u32[]{:S(2)}) copy-start(bf16[256,1280]{1,0:T(8,128)(2,1)S(1)} %collective-permute-done.refs_6_) | copy-start | bytes 1966084
  9.3 10.1 %copy-start = (bf16[1,1280,640]{2,1,0:T(8,128)(2,1)S(1)}, bf16[1,1280,640]{2,1,0:T(8,128)(2,1)}, u32[]{:S(2)}) copy-start(bf16[1,1280,640]{2,1,0:T(8,128)(2,1)} %param.10) | copy-start | bytes 4915204
  9.3 71.4 %all-to-all-start = ((bf16[32,48,1408]{2,1,0:T(8,128)(2,1)}), bf16[32,48,1408]{2,1,0:T(8,128)(2,1)}, u32[]{:S(2)}, u32[]{:S(2)}) async-start(bf16[32,48,1408]{2,1,0:T(8,128)(2,1)} %bitcast.26), calls=%async_computation | async-start | bytes 8650752 | tf_op jit(solution)/shard_map/all_to_all | solution.py:44
  104.1 52.3 %all-to-all-start.2 = ((bf16[32,112,512]{2,1,0:T(8,128)(2,1)}), bf16[32,112,512]{2,1,0:T(8,128)(2,1)}, u32[]{:S(2)}, u32[]{:S(2)}) async-start(bf16[32,112,512]{2,1,0:T(8,128)(2,1)} %get-tuple-element.27), calls=%async_computation.2 | async-start | bytes 7340032 | tf_op jit(solution)/shard_map/all_to_all | solution.py:44
  156.3 89.4 %all-to-all-start.1 = ((bf16[32,112,768]{2,1,0:T(8,128)(2,1)}), bf16[32,112,768]{2,1,0:T(8,128)(2,1)}, u32[]{:S(2)}, u32[]{:S(2)}) async-start(bf16[32,112,768]{2,1,0:T(8,128)(2,1)} %get-tuple-element.25), calls=%async_computation.1 | async-start | bytes 11010048 | tf_op jit(solution)/shard_map/all_to_all | solution.py:44
  172.1 73.7 %copy-start.1 = (bf16[256,1280]{1,0:T(8,128)(2,1)S(1)}, bf16[256,1280]{1,0:T(8,128)(2,1)}, u32[]{:S(2)}) copy-start(bf16[256,1280]{1,0:T(8,128)(2,1)} %query_side.1) | copy-start | bytes 1966084
  245.8 16.1 %collective-permute-start.1 = (bf16[256,1280]{1,0:T(8,128)(2,1)S(1)}, bf16[256,1280]{1,0:T(8,128)(2,1)S(1)}, u32[]{:S(2)}, u32[]{:S(2)}) collective-permute-start(bf16[256,1280]{1,0:T(8,128)(2,1)S(1)} %copy-done.1), channel_id=1, source_target_pairs={{0,3},{1,0},{2,1},{3,2},{4,7},{5,4},{6,5},{7,6},{8,11},{9,8},{10,9... | collective-permute-start | bytes 1966088 | tf_op jit(solution)/shard_map/ppermute | solution.py:40

commit v3 on v2

--- a/solution.py
+++ b/solution.py
@@ -9,8 +9,10 @@
 
 PAIR = 128
 CHUNKS = (2, 3)
-SLOTS, ROWS, TWICE = 48, 40, 24
-SENT = SLOTS + ROWS + TWICE
+ROWS, TWICE, SLOTS = 40, 24, 48
+GRADS = ROWS + TWICE
+SENT = GRADS + SLOTS
+STEP = 16
 SCALE = 0.125
 F32 = jnp.float32
 BF16 = jnp.bfloat16
@@ -44,7 +46,13 @@
     return lax.all_to_all(value, "dp", split_axis=0, concat_axis=0, tiled=True)
 
 
-def slots_along_lanes(dc, dr, capacity):
+def down_the_rows(dr):
+    filler = jnp.zeros((8 - dr.shape[0], dr.shape[1]), F32)
+    return jnp.concatenate([dr.astype(F32), filler], axis=0).T.astype(jnp.int32)
+
+
+def slots_along_lanes(dr, capacity):
+    dc = down_the_rows(dr)
     rows = dr.shape[1]
     shape = (rows, rows)
     before = lax.broadcasted_iota(jnp.int32, shape, 0) < lax.broadcasted_iota(
@@ -60,7 +68,8 @@
     return found
 
 
-def slots_along_sublanes(dc, dr, capacity):
+def slots_along_sublanes(dr, capacity):
+    dc = down_the_rows(dr)
     rows = dr.shape[1]
     shape = (rows, rows)
     before = lax.broadcasted_iota(jnp.int32, shape, 1) < lax.broadcasted_iota(
@@ -76,27 +85,37 @@
     return found
 
 
-def dispatch_kernel(capacity, dc_ref, dr_ref, own_ref, out_ref):
+def dispatch_kernel(capacity, dr_ref, own_ref, out_ref, slot_ref):
     rows = own_ref.shape[0]
+    block = pl.program_id(0)
+
+    @pl.when(block == 0)
+    def _():
+        for which, slot in enumerate(slots_along_lanes(dr_ref[...], capacity)):
+            slot_ref[which : which + 1, :] = slot
+
+    at = lax.broadcasted_iota(jnp.int32, (rows, rows), 0) + block * rows
+    table = jnp.logical_or(at == slot_ref[0:1, :], at == slot_ref[1:2, :])
+    table = jnp.where(table, 1.0, 0.0).astype(BF16)
     both = jnp.concatenate([own_ref[...], jnp.ones((rows, PAIR), BF16)], axis=1)
-    slot_a, slot_b = slots_along_lanes(dc_ref[...], dr_ref[...], capacity)
-    for block in range(out_ref.shape[0] // rows):
-        at = lax.broadcasted_iota(jnp.int32, (rows, rows), 0) + block * rows
-        table = jnp.logical_or(at == slot_a, at == slot_b)
-        table = jnp.where(table, 1.0, 0.0).astype(BF16)
-        out_ref[pl.ds(block * rows, rows), :] = mm(table, both).astype(BF16)
-
-
-def dispatch(capacity, readers, dc, dr, own):
+    out_ref[...] = mm(table, both).astype(BF16)
+
+
+def dispatch(capacity, readers, dr, own):
     rows, width = own.shape
     slots = readers * capacity
+    whole = lambda i: (0, 0)
     return pl.pallas_call(
         functools.partial(dispatch_kernel, capacity),
+        grid=(slots // rows,),
+        in_specs=[pl.BlockSpec(dr.shape, whole), pl.BlockSpec((rows, width), whole)],
+        out_specs=pl.BlockSpec((rows, width + PAIR), lambda i: (i, 0)),
         out_shape=jax.ShapeDtypeStruct((slots, width + PAIR), BF16),
-        compiler_params=params(),
+        scratch_shapes=[pltpu.VMEM((8, rows), jnp.int32)],
+        compiler_params=params(dimension_semantics=("arbitrary",)),
         cost_estimate=cost(2 * rows * width * slots, 2 * width * (rows + slots)),
         name="dispatch",
-    )(dc, dr, own)
+    )(dr, own)
 
 
 def attend_kernel(held, *refs):
@@ -127,12 +146,13 @@
             mem_t_ref[:, t * tile : (t + 1) * tile] = frames(t).T
         entering_t_ref[...] = entering_ref[...].T
 
+    for t in range(tiles):
+        kv_ref[pl.ds(t * tile, tile), :] = mm(frames(t), weights).astype(BF16)
+
     tops = []
     for t in range(tiles):
         at = pl.ds(t * tile, tile)
-        kv = mm(frames(t), weights).astype(BF16)
-        kv_ref[at, :] = kv
-        s = mm(kv[:, :PAIR], q_both, NT)
+        s = mm(kv_ref[at, :PAIR], q_both, NT)
         if t > 0:
             flag = got_ref[pl.ds((t - 1) * tile, tile), width : width + PAIR]
             s = s + (flag.astype(F32)[:, 0:1] - 1.0) * 1e30
@@ -173,15 +193,15 @@
         else:
             count = tile // SLOTS
             dkv = dkv.reshape(count, SLOTS, 2 * PAIR)
-            sent_ref[pl.ds((t - 1) * count, count), :SLOTS, :] = dkv
+            sent_ref[pl.ds((t - 1) * count, count), GRADS:, :] = dkv
     o_ref[...] = jnp.concatenate(out_t, axis=0).T.astype(BF16)
     dq = (jnp.concatenate(dq_t, axis=0) * SCALE).T.astype(BF16)
     dq_ref[...] = dq
     grad = mm(mem_t_ref[...], kv_ref[...]).reshape(readers, ROWS, 2 * PAIR)
-    sent_ref[:, SLOTS : SLOTS + ROWS, :] = grad.astype(BF16)
+    sent_ref[:, :ROWS, :] = grad.astype(BF16)
     grad = mm(entering_t_ref[...], dq).reshape(readers, ROWS, PAIR)
     grad = jnp.concatenate([grad[:, :TWICE], grad[:, ROWS - TWICE :]], axis=2)
-    sent_ref[:, SLOTS + ROWS :, :] = grad.astype(BF16)
+    sent_ref[:, ROWS:GRADS, :] = grad.astype(BF16)
 
 
 def attend(first, pairs, readers, queries, cot, own, got, wk, wv, entering, filled):
@@ -250,101 +270,123 @@
     )(dq, wq)
 
 
-def combine_kernel(first, capacity, last, dc_ref, dr_ref, down_ref, back_ref, wk_ref, wv_ref, *refs):
-    held, out_ref = refs[:-1], refs[-1]
-    rows = down_ref.shape[0]
-    lanes = back_ref.shape[2]
-    slot_a, slot_b = slots_along_sublanes(dc_ref[...], dr_ref[...], capacity)
-    tot = down_ref[:, 2 * first * PAIR : 2 * first * PAIR + lanes].astype(F32)
-    count = rows // SLOTS
-    for block in range(back_ref.shape[0] // count):
+def table_kernel(capacity, dr_ref, out_ref):
+    rows = out_ref.shape[0]
+    slot_a, slot_b = slots_along_sublanes(dr_ref[...], capacity)
+    for block in range(out_ref.shape[1] // rows):
         at = lax.broadcasted_iota(jnp.int32, (rows, rows), 1) + block * rows
         table = jnp.logical_or(at == slot_a, at == slot_b)
-        table = jnp.where(table, 1.0, 0.0).astype(BF16)
-        part = back_ref[pl.ds(block * count, count), :, :].reshape(rows, lanes)
-        tot = tot + mm(table, part)
-    tot = tot.astype(BF16)
-    pieces = [tot[:, c * PAIR : (c + 1) * PAIR] for c in range(lanes // PAIR)]
-    cut = slice(first * PAIR, first * PAIR + lanes // 2)
-    out = mm(jnp.concatenate(pieces[0::2], axis=1), wk_ref[:, cut], NT)
-    out = out + mm(jnp.concatenate(pieces[1::2], axis=1), wv_ref[:, cut], NT)
-    for r in held:
-        out = out + r[...]
-    out_ref[...] = out.astype(out_ref.dtype)
-
-
-def combine(first, last, capacity, dc, dr, down, back, wk, wv, held):
+        out_ref[:, block * rows : (block + 1) * rows] = jnp.where(table, 1.0, 0.0).astype(BF16)
+
+
+def table_of(capacity, readers, dr):
+    shape = (dr.shape[1], readers * capacity)
+    return pl.pallas_call(
+        functools.partial(table_kernel, capacity),
+        out_shape=jax.ShapeDtypeStruct(shape, BF16),
+        compiler_params=params(),
+        cost_estimate=cost(0, 2 * shape[0] * shape[1]),
+        name="table_of",
+    )(dr)
+
+
+def combine_kernel(held, table_ref, down_ref, wk_ref, wv_ref, *refs):
+    views = refs[: SLOTS // STEP]
+    out_ref, sum_ref = refs[-2:]
+    lanes = down_ref.shape[1]
+    p = pl.program_id(0)
+    back = jnp.concatenate([v[...] for v in views], axis=1).reshape(-1, lanes)
+    tot = (down_ref[...].astype(F32) + mm(table_ref[...], back)).astype(BF16)
+    weights = jnp.concatenate([wk_ref[...], wv_ref[...]], axis=1)
+    out = mm(tot, weights, NT)
+
+    @pl.when(p == 0)
+    def _():
+        sum_ref[...] = out + refs[SLOTS // STEP][...] if held else out
+
+    @pl.when(p > 0)
+    def _():
+        sum_ref[...] += out
+
+    @pl.when(p == pl.num_programs(0) - 1)
+    def _():
+        out_ref[...] = sum_ref[...].astype(out_ref.dtype)
+
+
+def combine(first, last, table, down, back, wk, wv, held):
     rows = down.shape[0]
-    width, heads = wk.shape
+    width = wk.shape[0]
     readers, _, lanes = back.shape
-    whole = lambda i: (0, 0)
+    pairs = lanes // (2 * PAIR)
+    whole = lambda p: (0, 0)
+    pair_at = lambda p: (0, first + p)
     full = lambda a: pl.BlockSpec(a.shape, whole)
-    return pl.pallas_call(
-        functools.partial(combine_kernel, first, capacity, last),
-        grid=(1,),
+    view = lambda i: pl.BlockSpec((readers, STEP, 2 * PAIR), lambda p: (0, GRADS // STEP + i, p))
+    return pl.pallas_call(
+        functools.partial(combine_kernel, len(held)),
+        grid=(pairs,),
         in_specs=[
-            full(dc),
-            full(dr),
-            full(down),
-            pl.BlockSpec((readers, SLOTS, lanes), lambda i: (0, 0, 0)),
-            full(wk),
-            full(wv),
+            full(table),
+            pl.BlockSpec((rows, 2 * PAIR), pair_at),
+            pl.BlockSpec((width, PAIR), pair_at),
+            pl.BlockSpec((width, PAIR), pair_at),
         ]
+        + [view(i) for i in range(SLOTS // STEP)]
         + [full(h) for h in held],
         out_specs=pl.BlockSpec((rows, width), whole),
         out_shape=jax.ShapeDtypeStruct((rows, width), BF16 if last else F32),
-        compiler_params=params(),
+        scratch_shapes=[pltpu.VMEM((rows, width), F32)],
+        compiler_params=params(dimension_semantics=("arbitrary",)),
         cost_estimate=cost(
             2 * rows * lanes * (width + readers * SLOTS),
             2 * (rows * width + width * lanes + readers * SLOTS * lanes),
         ),
         name=f"combine_{first}",
-    )(dc, dr, down, back, wk, wv, *held)
-
-
-def sum_kernel(back_ref, out_ref):
-    sums = [back_ref[a].astype(F32) for a in range(4)]
-    for a in range(4, back_ref.shape[0]):
-        sums[a % 4] = sums[a % 4] + back_ref[a].astype(F32)
-    out_ref[...] = (sums[0] + sums[1]) + (sums[2] + sums[3])
-
-
-def summed(first, back):
-    readers, rows, lanes = back.shape
-    step = 16
-    return pl.pallas_call(
-        sum_kernel,
-        grid=((rows - SLOTS) // step,),
-        in_specs=[pl.BlockSpec((readers, step, lanes), lambda i: (0, SLOTS // step + i, 0))],
-        out_specs=pl.BlockSpec((step, lanes), lambda i: (i, 0)),
-        out_shape=jax.ShapeDtypeStruct((rows - SLOTS, lanes), F32),
+    )(table, down, wk, wv, *([back] * (SLOTS // STEP)), *held)
+
+
+def sum_kernel(last, back_ref, *refs):
+    held, out_ref = refs[:-1], refs[-1]
+
+    def added(lanes):
+        sums = [back_ref[a, :, lanes].astype(F32) for a in range(4)]
+        for a in range(4, back_ref.shape[0]):
+            sums[a % 4] = sums[a % 4] + back_ref[a, :, lanes].astype(F32)
+        return (sums[0] + sums[1]) + (sums[2] + sums[3])
+
+    mine = [added(slice(c, c + PAIR)) for c in range(0, back_ref.shape[2], PAIR)]
+    if not last:
+        out_ref[...] = jnp.concatenate(mine, axis=1)
+        return
+    pieces = []
+    for r in held:
+        pieces += [r[:, c : c + PAIR] for c in range(0, r.shape[1], PAIR)]
+    pieces += mine
+    heads = out_ref.shape[1] // 3
+    for p in range(heads // PAIR):
+        upper, lower = pieces[2 * p], pieces[2 * p + 1]
+        at = slice(p * PAIR, (p + 1) * PAIR)
+        out_ref[:TWICE, at] = upper[ROWS:]
+        out_ref[TWICE:, at] = lower[2 * TWICE :]
+        out_ref[:, heads + p * PAIR : heads + (p + 1) * PAIR] = upper[:ROWS]
+        out_ref[:, 2 * heads + p * PAIR : 2 * heads + (p + 1) * PAIR] = lower[:ROWS]
+
+
+def summed(first, last, heads, back, held):
+    readers, _, lanes = back.shape
+    shape = (ROWS, 3 * heads) if last else (GRADS, lanes)
+    whole = lambda i: (0, 0)
+    return pl.pallas_call(
+        functools.partial(sum_kernel, last),
+        grid=(1,),
+        in_specs=[pl.BlockSpec((readers, GRADS, lanes), lambda i: (0, 0, 0))]
+        + [pl.BlockSpec(h.shape, whole) for h in held],
+        out_specs=pl.BlockSpec(shape, whole),
+        out_shape=jax.ShapeDtypeStruct(shape, F32),
         compiler_params=params(),
-        cost_estimate=cost(readers * rows * lanes, 2 * readers * rows * lanes),
+        cost_estimate=cost(readers * GRADS * lanes, 2 * readers * GRADS * lanes),
         name=f"summed_{first}",
-    )(back)
-
-
-def gather_kernel(*refs):
-    parts, out_ref = refs[:-1], refs[-1]
-    heads = out_ref.shape[1] // 3
-    both = jnp.concatenate([r[...] for r in parts], axis=1)
-    pieces = [both[:, c * PAIR : (c + 1) * PAIR] for c in range(2 * heads // PAIR)]
-    upper = jnp.concatenate(pieces[0::2], axis=1)
-    lower = jnp.concatenate(pieces[1::2], axis=1)
-    out_ref[:TWICE, :heads] = upper[ROWS:]
-    out_ref[TWICE:, :heads] = lower[2 * TWICE :]
-    out_ref[:, heads : 2 * heads] = upper[:ROWS]
-    out_ref[:, 2 * heads :] = lower[:ROWS]
-
-
-def gathered(heads, parts):
-    return pl.pallas_call(
-        gather_kernel,
-        out_shape=jax.ShapeDtypeStruct((ROWS, 3 * heads), F32),
-        compiler_params=params(),
-        cost_estimate=cost(0, 24 * ROWS * heads),
-        name="gathered",
-    )(*parts)
+    )(back, *held)
 
 
 def per_device(encoder, destinations, hidden, w_query, w_key, w_value, cotangent):
@@ -356,14 +398,13 @@
     heads = wq.shape[1]
     readers = lax.axis_size("dp")
     capacity = 4 * rows // readers
-    dest_rows = dest.T
 
     slots = readers * capacity
 
     slots = readers * capacity
 
     entering = passed_along(hidden[0, 0], "section", 1)
-    out = dispatch(capacity, readers, dest, dest_rows, own)
+    out = dispatch(capacity, readers, dest.T, own)
     out, entering = lax.optimization_barrier((out, entering))
     queries = jnp.dot(entering, wq, preferred_element_type=F32).astype(BF16)
     got = exchanged(out.reshape(readers, capacity, -1)).reshape(slots, -1)
@@ -373,26 +414,26 @@
         *filled, sent = attend(
             first, pairs, readers, queries, cot, own, got, wk, wv, entering, filled
         )
-        backs.append(exchanged(sent))
         firsts.append(first)
         first += pairs
+        backs.append(exchanged(sent))
     attended, dq, down = filled
     dentering = query_side(dq, wq)
+    table = table_of(capacity, readers, dest.T)
+
     held, grads = [], []
     for c, first in enumerate(firsts):
         last = c == len(firsts) - 1
         if held:
-            backs[c], held, grads, down, dentering = lax.optimization_barrier(
-                (backs[c], held, grads, down, dentering)
+            backs[c], held, grads, down, dentering, table = lax.optimization_barrier(
+                (backs[c], held, grads, down, dentering, table)
             )
         if last:
             d_hidden = passed_along(dentering, "section", -1)
-        held = [
-            combine(first, last, capacity, dest, dest_rows, down, backs[c], wk, wv, held)
-        ]
-        grads.append(summed(first, backs[c]))
+        held = [combine(first, last, table, down, backs[c], wk, wv, held)]
+        grads.append(summed(first, last, heads, backs[c], grads))
     d_enc = held[0]
-    grads = gathered(heads, grads)
+    grads = grads[-1]
     return (attended[None, None], d_hidden[None, None], d_enc[None, None], grads[None])
 
 

time: 263 us -> 256 us (0.973)
  Pallas kernels: 89.4 us -> 76.4 us
  waiting for transfers between devices: 142 us -> 149 us
    pallas_call x2, Pallas kernels: 55.7 us -> 45.3 us  [attend(): pl.pallas_call(functools.partial(attend_kernel, len(filled)), grid=(pairs...]
    all_to_all x3, waiting for transfers between devices: 141 us -> 147 us  [exchanged(): return lax.all_to_all(value, 'dp', split_axis=0, concat_axis=0, tiled=True)]
    pallas_call x6, Pallas kernels: 30.7 us -> 28 us  [the longest x2 14 us: combine(): pl.pallas_call(functools.partial(combine_kernel, len(held)), grid=(pairs,...]
  transfers between devices with their start and end apart: 5 -> 5, of which waited for: 4 -> 4; matrix products, arithmetic and copies ran while one was open for 1% -> 1% of each run, Pallas kernels for 25% -> 22%
where the time goes in v3:
time: 256 us; the launch traced here: 255 us
  waiting for transfers between devices  149 us (58%)
  Pallas kernels  76.4 us (30%)
  starting transfers between devices  27.1 us (11%)
    all_to_all x3, waiting for transfers between devices, exchanged(): return lax.all_to_all(value, 'dp', split_axis=0, concat_axis=0, tiled=True)  147 us
    pallas_call x2, Pallas kernels, attend(): pl.pallas_call(functools.partial(attend_kernel, len(filled)), grid=(pairs...  45.3 us
    all_to_all x3, starting transfers between devices, exchanged(): return lax.all_to_all(value, 'dp', split_axis=0, concat_axis=0, tiled=True)  24.5 us
    pallas_call x2, Pallas kernels, combine(): pl.pallas_call(functools.partial(combine_kernel, len(held)), grid=(pairs,...  14 us
    pallas_call x1, Pallas kernels, dispatch(): pl.pallas_call(functools.partial(dispatch_kernel, capacity), grid=(slots...  5.88 us
    pallas_call x2, Pallas kernels, summed(): pl.pallas_call(functools.partial(sum_kernel, last), grid=(1,), in_specs=[...  5.53 us
  transfers between devices with their start and end apart: 5, of which 4 were waited for; matrix products, arithmetic and copies ran while one was open for 1% of the time, Pallas kernels for 22%

profile of v3, /device:TPU:11, one launch (start us, length us, event | category | flops | bytes accessed | tf_op | source)
XLA Modules:
  0.0 255.1 jit_solution(11145703315042801386)
XLA Ops:
  0.6 0.8 collective-permute-start
  1.4 5.9 %dispatch.1 = bf16[1536,1408]{1,0:T(8,128)(2,1)} custom-call(s32[2,384]{1,0:T(2,128)} %bitcast.31, bf16[384,1280]{1,0:T(8,128)(2,1)} %bitcast.33), custom_call_target="tpu_custom_call" | custom-call | flops 1509949440 | bytes 4915200 | tf_op jit(solution)/shard_map/dispatch/pallas_call | solution.py:108
  7.3 2.0 collective-permute-done.refs_6_
  9.3 0.0 copy-start.2
  9.3 0.0 copy-start
  9.3 10.1 %all-to-all-start = ((bf16[32,48,1408]{2,1,0:T(8,128)(2,1)}), bf16[32,48,1408]{2,1,0:T(8,128)(2,1)}, u32[]{:S(2)}, u32[]{:S(2)}) async-start(bf16[32,48,1408]{2,1,0:T(8,128)(2,1)} %bitcast.26), calls=%async_computation | async-start | bytes 8650752 | tf_op jit(solution)/shard_map/all_to_all | solution.py:46
  19.4 0.0 copy-done.2
  19.4 0.0 copy-done
  19.4 1.4 convolution_convert_fusion.refs_0_
  20.8 59.8 %all-to-all-done = bf16[32,48,1408]{2,1,0:T(8,128)(2,1)} async-done(((bf16[32,48,1408]{2,1,0:T(8,128)(2,1)}), bf16[32,48,1408]{2,1,0:T(8,128)(2,1)}, u32[]{:S(2)}, u32[]{:S(2)}) %all-to-all-start) | async-done | bytes 4325408 | tf_op jit(solution)/shard_map/all_to_all | solution.py:46
  80.6 19.2 %attend_0.1 = (bf16[256,640]{1,0:T(8,128)(2,1)}, bf16[256,640]{1,0:T(8,128)(2,1)}, bf16[384,1280]{1,0:T(8,128)(2,1)}, bf16[32,112,512]{2,1,0:T(8,128)(2,1)}) custom-call(bf16[256,640]{1,0:T(8,128)(2,1)} %convolution_convert_fusion.refs_0_, bf16[256,640]{1,0:T(8,128)(2,1)} %bitcast.37, bf16[384,1280]{1,0:T(8,128)(2,1)} %bitcast.34, ...), custom_call_target="tpu_custom_call" | custom-call | flops 11072962560 | bytes 10813440 | tf_op jit(solution)/shard_map/attend_0/pallas_call | solution.py:214
  99.9 5.4 %all-to-all-start.2 = ((bf16[32,112,512]{2,1,0:T(8,128)(2,1)}), bf16[32,112,512]{2,1,0:T(8,128)(2,1)}, u32[]{:S(2)}, u32[]{:S(2)}) async-start(bf16[32,112,512]{2,1,0:T(8,128)(2,1)} %get-tuple-element.28), calls=%async_computation.2 | async-start | bytes 7340032 | tf_op jit(solution)/shard_map/all_to_all | solution.py:46
  105.2 26.1 %attend_2.1 = (bf16[256,640]{1,0:T(8,128)(2,1)}, bf16[256,640]{1,0:T(8,128)(2,1)}, bf16[384,1280]{1,0:T(8,128)(2,1)}, bf16[32,112,768]{2,1,0:T(8,128)(2,1)}) custom-call(bf16[256,640]{1,0:T(8,128)(2,1)} %convolution_convert_fusion.refs_0_, bf16[256,640]{1,0:T(8,128)(2,1)} %bitcast.38, ...), custom_call_target="tpu_custom_call", output_to_operand_aliasing={{0}: (7, {}), {1}: (8, {}), {2}: (9, {})} | custom-call | flops 16609443840 | bytes 13762560 | tf_op jit(solution)/shard_map/attend_2/pallas_call | solution.py:214
  131.3 20.9 %all-to-all-done.2.refs_0_.refs_1_.refs_2_.back_ref = bf16[32,112,512]{2,1,0:T(8,128)(2,1)} async-done(((bf16[32,112,512]{2,1,0:T(8,128)(2,1)}), bf16[32,112,512]{2,1,0:T(8,128)(2,1)}, u32[]{:S(2)}, u32[]{:S(2)}) %all-to-all-start.2) | async-done | bytes 3670048 | tf_op jit(solution)/shard_map/all_to_all | solution.py:46
  152.2 9.0 %all-to-all-start.1 = ((bf16[32,112,768]{2,1,0:T(8,128)(2,1)}), bf16[32,112,768]{2,1,0:T(8,128)(2,1)}, u32[]{:S(2)}, u32[]{:S(2)}) async-start(bf16[32,112,768]{2,1,0:T(8,128)(2,1)} %get-tuple-element.26), calls=%async_computation.1 | async-start | bytes 11010048 | tf_op jit(solution)/shard_map/all_to_all | solution.py:46
  161.3 2.6 %table_of.1.table_ref = bf16[384,1536]{1,0:T(8,128)(2,1)} custom-call(s32[2,384]{1,0:T(2,128)} %bitcast.32), custom_call_target="tpu_custom_call" | custom-call | bytes 1179648 | tf_op jit(solution)/shard_map/table_of/pallas_call | solution.py:284
  163.8 3.1 %query_side.1 = bf16[256,1280]{1,0:T(8,128)(2,1)} custom-call(bf16[256,640]{1,0:T(8,128)(2,1)} %get-tuple-element.29.dq_ref, bf16[1280,640]{1,0:T(8,128)(2,1)} %bitcast.27), custom_call_target="tpu_custom_call" | custom-call | flops 419430400 | bytes 2293760 | tf_op jit(solution)/shard_map/query_side/pallas_call | solution.py:264
  166.9 2.5 summed_0.1.refs_0_
  169.5 0.0 copy-start.1
  169.5 6.1 %combine_0.1.refs_3_ = f32[384,1280]{1,0:T(8,128)} custom-call(bf16[384,1536]{1,0:T(8,128)(2,1)} %table_of.1.table_ref, bf16[384,1280]{1,0:T(8,128)(2,1)} %get-tuple-element.32.down_ref, bf16[1280,640]{1,0:T(8,128)(2,1)} %bitcast.20, bf16[1280,640]{1,0:T(8,128)(2,1)} %bitcast.24, bf16[32,112,512]{2,1,0:T(8,128)(2,1)} %all-to-all-done.2.refs_0_.refs_1_.refs_2_.back_ref, ...), custom_call_target="tpu_custom_call" | custom-call | flops 1107296256 | bytes 3866624 | tf_op jit(solution)/shard_map/combine_0/pallas_call | solution.py:325
  175.6 66.0 %all-to-all-done.1.refs_0_.refs_1_.refs_2_.back_ref = bf16[32,112,768]{2,1,0:T(8,128)(2,1)} async-done(((bf16[32,112,768]{2,1,0:T(8,128)(2,1)}), bf16[32,112,768]{2,1,0:T(8,128)(2,1)}, u32[]{:S(2)}, u32[]{:S(2)}) %all-to-all-start.1) | async-done | bytes 5505056 | tf_op jit(solution)/shard_map/all_to_all | solution.py:46
  241.6 0.0 copy-done.1
  241.6 1.8 collective-permute-start.1
  243.3 3.0 %summed_2.1 = f32[40,1920]{1,0:T(8,128)} custom-call(bf16[32,112,768]{2,1,0:T(8,128)(2,1)} %all-to-all-done.1.refs_0_.refs_1_.refs_2_.back_ref, f32[64,512]{1,0:T(8,128)} %summed_0.1.refs_0_), custom_call_target="tpu_custom_call" | custom-call | flops 1572864 | bytes 3145728 | tf_op jit(solution)/shard_map/summed_2/pallas_call | solution.py:379
  246.4 7.9 %combine_2.1 = bf16[384,1280]{1,0:T(8,128)(2,1)} custom-call(bf16[384,1536]{1,0:T(8,128)(2,1)} %table_of.1.table_ref, bf16[384,1280]{1,0:T(8,128)(2,1)} %get-tuple-element.32.down_ref, bf16[1280,640]{1,0:T(8,128)(2,1)} %bitcast.21, bf16[1280,640]{1,0:T(8,128)(2,1)} %bitcast.25, bf16[32,112,768]{2,1,0:T(8,128)(2,1)} %all-to-all-done.1.refs_0_.refs_1_.refs_2_.back_ref, ...), custom_call_target="tpu_custom_call" | custom-call | flops 1660944384 | bytes 5308416 | tf_op jit(solution)/shard_map/combine_2/pallas_call | solution.py:325
  254.3 0.0 collective-permute-done.1
  254.3 0.8 copy.18
Async XLA Ops:
  0.6 8.6 %collective-permute-start = (bf16[256,1280]{1,0:T(8,128)(2,1)}, bf16[256,1280]{1,0:T(8,128)(2,1)S(1)}, u32[]{:S(2)}, u32[]{:S(2)}) collective-permute-start(bf16[256,1280]{1,0:T(8,128)(2,1)} %bitcast.36), channel_id=1, source_target_pairs={{0,1},{1,2},{2,3},{3,0},{4,5},{5,6},{6,7},{7,4},{8,9},{9,10},{10,1... | collective-permute-start | bytes 1966088 | tf_op jit(solution)/shard_map/ppermute | solution.py:42
  9.3 10.1 %copy-start.2 = (bf16[256,1280]{1,0:T(8,128)(2,1)}, bf16[256,1280]{1,0:T(8,128)(2,1)S(1)}, u32[]{:S(2)}) copy-start(bf16[256,1280]{1,0:T(8,128)(2,1)S(1)} %collective-permute-done.refs_6_) | copy-start | bytes 1966084
  9.3 10.1 %copy-start = (bf16[1,1280,640]{2,1,0:T(8,128)(2,1)S(1)}, bf16[1,1280,640]{2,1,0:T(8,128)(2,1)}, u32[]{:S(2)}) copy-start(bf16[1,1280,640]{2,1,0:T(8,128)(2,1)} %param.10) | copy-start | bytes 4915204
  9.3 71.3 %all-to-all-start = ((bf16[32,48,1408]{2,1,0:T(8,128)(2,1)}), bf16[32,48,1408]{2,1,0:T(8,128)(2,1)}, u32[]{:S(2)}, u32[]{:S(2)}) async-start(bf16[32,48,1408]{2,1,0:T(8,128)(2,1)} %bitcast.26), calls=%async_computation | async-start | bytes 8650752 | tf_op jit(solution)/shard_map/all_to_all | solution.py:46
  99.9 52.3 %all-to-all-start.2 = ((bf16[32,112,512]{2,1,0:T(8,128)(2,1)}), bf16[32,112,512]{2,1,0:T(8,128)(2,1)}, u32[]{:S(2)}, u32[]{:S(2)}) async-start(bf16[32,112,512]{2,1,0:T(8,128)(2,1)} %get-tuple-element.28), calls=%async_computation.2 | async-start | bytes 7340032 | tf_op jit(solution)/shard_map/all_to_all | solution.py:46
  152.2 89.4 %all-to-all-start.1 = ((bf16[32,112,768]{2,1,0:T(8,128)(2,1)}), bf16[32,112,768]{2,1,0:T(8,128)(2,1)}, u32[]{:S(2)}, u32[]{:S(2)}) async-start(bf16[32,112,768]{2,1,0:T(8,128)(2,1)} %get-tuple-element.26), calls=%async_computation.1 | async-start | bytes 11010048 | tf_op jit(solution)/shard_map/all_to_all | solution.py:46
  169.5 72.1 %copy-start.1 = (bf16[256,1280]{1,0:T(8,128)(2,1)S(1)}, bf16[256,1280]{1,0:T(8,128)(2,1)}, u32[]{:S(2)}) copy-start(bf16[256,1280]{1,0:T(8,128)(2,1)} %query_side.1) | copy-start | bytes 1966084
  241.6 12.7 %collective-permute-start.1 = (bf16[256,1280]{1,0:T(8,128)(2,1)S(1)}, bf16[256,1280]{1,0:T(8,128)(2,1)S(1)}, u32[]{:S(2)}, u32[]{:S(2)}) collective-permute-start(bf16[256,1280]{1,0:T(8,128)(2,1)S(1)} %copy-done.1), channel_id=1, source_target_pairs={{0,3},{1,0},{2,1},{3,2},{4,7},{5,4},{6,5},{7,6},{8,11},{9,8},{10,9... | collective-permute-start | bytes 1966088 | tf_op jit(solution)/shard_map/ppermute | solution.py:42

commit v4 on v3

--- a/solution.py
+++ b/solution.py
@@ -17,6 +17,7 @@
 F32 = jnp.float32
 BF16 = jnp.bfloat16
 VMEM_LIMIT = 60 * 1024 * 1024
+SMALL = 20 * 1024 * 1024
 
 NT = (((1,), (1,)), ((), ()))
 NN = (((1,), (0,)), ((), ()))
@@ -26,8 +27,8 @@
     return lax.dot_general(a, b, dims, preferred_element_type=F32)
 
 
-def params(**kw):
-    return pltpu.CompilerParams(vmem_limit_bytes=VMEM_LIMIT, **kw)
+def params(grant=VMEM_LIMIT, **kw):
+    return pltpu.CompilerParams(vmem_limit_bytes=grant, **kw)
 
 
 def cost(flops, bytes_accessed, transcendentals=0):
@@ -264,7 +265,7 @@
     return pl.pallas_call(
         query_kernel,
         out_shape=jax.ShapeDtypeStruct((dec, width), BF16),
-        compiler_params=params(),
+        compiler_params=params(SMALL),
         cost_estimate=cost(2 * dec * width * heads, 2 * width * (dec + heads)),
         name="query_side",
     )(dq, wq)
@@ -284,7 +285,7 @@
     return pl.pallas_call(
         functools.partial(table_kernel, capacity),
         out_shape=jax.ShapeDtypeStruct(shape, BF16),
-        compiler_params=params(),
+        compiler_params=params(SMALL),
         cost_estimate=cost(0, 2 * shape[0] * shape[1]),
         name="table_of",
     )(dr)
@@ -336,7 +337,7 @@
         out_specs=pl.BlockSpec((rows, width), whole),
         out_shape=jax.ShapeDtypeStruct((rows, width), BF16 if last else F32),
         scratch_shapes=[pltpu.VMEM((rows, width), F32)],
-        compiler_params=params(dimension_semantics=("arbitrary",)),
+        compiler_params=params(SMALL, dimension_semantics=("arbitrary",)),
         cost_estimate=cost(
             2 * rows * lanes * (width + readers * SLOTS),
             2 * (rows * width + width * lanes + readers * SLOTS * lanes),
@@ -383,7 +384,7 @@
         + [pl.BlockSpec(h.shape, whole) for h in held],
         out_specs=pl.BlockSpec(shape, whole),
         out_shape=jax.ShapeDtypeStruct(shape, F32),
-        compiler_params=params(),
+        compiler_params=params(SMALL),
         cost_estimate=cost(readers * GRADS * lanes, 2 * readers * GRADS * lanes),
         name=f"summed_{first}",
     )(back, *held)
@@ -405,7 +406,6 @@
 
     entering = passed_along(hidden[0, 0], "section", 1)
     out = dispatch(capacity, readers, dest.T, own)
-    out, entering = lax.optimization_barrier((out, entering))
     queries = jnp.dot(entering, wq, preferred_element_type=F32).astype(BF16)
     got = exchanged(out.reshape(readers, capacity, -1)).reshape(slots, -1)
 

time: 256 us -> 268 us (1.047)
  waiting for transfers between devices: 149 us -> 158 us
  Pallas kernels: 76.4 us -> 68.9 us
  starting transfers between devices: 27.1 us -> 33.3 us
    ppermute x2, waiting for transfers between devices: 1.97 us -> 36.6 us  [passed_along(): return lax.ppermute(value, axis, pairs)]
    all_to_all x3, waiting for transfers between devices: 147 us -> 122 us  [exchanged(): return lax.all_to_all(value, 'dp', split_axis=0, concat_axis=0, tiled=True)]
    all_to_all x3, starting transfers between devices: 24.5 us -> 30 us  [exchanged(): return lax.all_to_all(value, 'dp', split_axis=0, concat_axis=0, tiled=True)]
    pallas_call x2, Pallas kernels: 14 us -> 10.9 us  [combine(): pl.pallas_call(functools.partial(combine_kernel, len(held)), grid=(pairs,...]
  transfers between devices with their start and end apart: 5 -> 5, of which waited for: 4 -> 4; matrix products, arithmetic and copies ran while one was open for 1% -> 1% of each run, Pallas kernels for 22% -> 17%
where the time goes in v4:
time: 268 us; the launch traced here: 265 us
  waiting for transfers between devices  158 us (59%)
  Pallas kernels  68.9 us (26%)
  starting transfers between devices  33.3 us (12%)
    all_to_all x3, waiting for transfers between devices, exchanged(): return lax.all_to_all(value, 'dp', split_axis=0, concat_axis=0, tiled=True)  122 us
    pallas_call x2, Pallas kernels, attend(): pl.pallas_call(functools.partial(attend_kernel, len(filled)), grid=(pairs...  45.3 us
    ppermute x2, waiting for transfers between devices, passed_along(): return lax.ppermute(value, axis, pairs)  36.6 us
    all_to_all x3, starting transfers between devices, exchanged(): return lax.all_to_all(value, 'dp', split_axis=0, concat_axis=0, tiled=True)  30 us
    pallas_call x2, Pallas kernels, combine(): pl.pallas_call(functools.partial(combine_kernel, len(held)), grid=(pairs,...  10.9 us
    pallas_call x1, Pallas kernels, dispatch(): pl.pallas_call(functools.partial(dispatch_kernel, capacity), grid=(slots...  5.89 us
  transfers between devices with their start and end apart: 5, of which 4 were waited for; matrix products, arithmetic and copies ran while one was open for 1% of the time, Pallas kernels for 17%

profile of v4, /device:TPU:11, one launch (start us, length us, event | category | flops | bytes accessed | tf_op | source)
XLA Modules:
  0.0 264.8 jit_solution(11870541947361470550)
XLA Ops:
  0.6 5.9 %dispatch.1 = bf16[1536,1408]{1,0:T(8,128)(2,1)} custom-call(s32[2,384]{1,0:T(2,128)} %bitcast.27, bf16[384,1280]{1,0:T(8,128)(2,1)} %bitcast.33), custom_call_target="tpu_custom_call" | custom-call | flops 1509949440 | bytes 4915200 | tf_op jit(solution)/shard_map/dispatch/pallas_call | solution.py:109
  6.5 0.0 copy-start.10
  6.5 0.0 copy-start.6
  6.5 9.8 %all-to-all-start = ((bf16[32,48,1408]{2,1,0:T(8,128)(2,1)}), bf16[32,48,1408]{2,1,0:T(8,128)(2,1)}, u32[]{:S(2)}, u32[]{:S(2)}) async-start(bf16[32,48,1408]{2,1,0:T(8,128)(2,1)} %bitcast.29), calls=%async_computation | async-start | bytes 8650752 | tf_op jit(solution)/shard_map/all_to_all | solution.py:47
  16.4 0.0 copy-done.10
  16.4 2.3 collective-permute-start
  18.6 36.6 %collective-permute-done.refs_6_ = bf16[256,1280]{1,0:T(8,128)(2,1)S(1)} collective-permute-done((bf16[256,1280]{1,0:T(8,128)(2,1)S(1)}, bf16[256,1280]{1,0:T(8,128)(2,1)S(1)}, u32[]{:S(2)}, u32[]{:S(2)}) %collective-permute-start) | collective-permute-done | bytes 655392 | tf_op jit(solution)/shard_map/ppermute | solution.py:43
  55.2 0.0 copy-done.6
  55.2 0.0 copy-start.11
  55.2 1.4 convolution_convert_fusion.refs_0_
  56.6 20.2 %all-to-all-done = bf16[32,48,1408]{2,1,0:T(8,128)(2,1)} async-done(((bf16[32,48,1408]{2,1,0:T(8,128)(2,1)}), bf16[32,48,1408]{2,1,0:T(8,128)(2,1)}, u32[]{:S(2)}, u32[]{:S(2)}) %all-to-all-start) | async-done | bytes 4325408 | tf_op jit(solution)/shard_map/all_to_all | solution.py:47
  76.8 0.0 copy-done.11
  76.8 19.2 %attend_0.1 = (bf16[256,640]{1,0:T(8,128)(2,1)}, bf16[256,640]{1,0:T(8,128)(2,1)}, bf16[384,1280]{1,0:T(8,128)(2,1)}, bf16[32,112,512]{2,1,0:T(8,128)(2,1)}) custom-call(bf16[256,640]{1,0:T(8,128)(2,1)} %convolution_convert_fusion.refs_0_, bf16[256,640]{1,0:T(8,128)(2,1)} %bitcast.37, bf16[384,1280]{1,0:T(8,128)(2,1)} %bitcast.34, ...), custom_call_target="tpu_custom_call" | custom-call | flops 11072962560 | bytes 10813440 | tf_op jit(solution)/shard_map/attend_0/pallas_call | solution.py:215
  96.0 15.2 %all-to-all-start.2 = ((bf16[32,112,512]{2,1,0:T(8,128)(2,1)}), bf16[32,112,512]{2,1,0:T(8,128)(2,1)}, u32[]{:S(2)}, u32[]{:S(2)}) async-start(bf16[32,112,512]{2,1,0:T(8,128)(2,1)} %get-tuple-element.24), calls=%async_computation.2 | async-start | bytes 7340032 | tf_op jit(solution)/shard_map/all_to_all | solution.py:47
  111.2 26.1 %attend_2.1 = (bf16[256,640]{1,0:T(8,128)(2,1)}, bf16[256,640]{1,0:T(8,128)(2,1)}, bf16[384,1280]{1,0:T(8,128)(2,1)}, bf16[32,112,768]{2,1,0:T(8,128)(2,1)}) custom-call(bf16[256,640]{1,0:T(8,128)(2,1)} %convolution_convert_fusion.refs_0_, bf16[256,640]{1,0:T(8,128)(2,1)} %bitcast.38, ...), custom_call_target="tpu_custom_call", output_to_operand_aliasing={{0}: (7, {}), {1}: (8, {}), {2}: (9, {})} | custom-call | flops 16609443840 | bytes 13762560 | tf_op jit(solution)/shard_map/attend_2/pallas_call | solution.py:215
  137.3 27.0 %all-to-all-done.2.refs_0_.refs_1_.refs_2_.back_ref = bf16[32,112,512]{2,1,0:T(8,128)(2,1)} async-done(((bf16[32,112,512]{2,1,0:T(8,128)(2,1)}), bf16[32,112,512]{2,1,0:T(8,128)(2,1)}, u32[]{:S(2)}, u32[]{:S(2)}) %all-to-all-start.2) | async-done | bytes 3670048 | tf_op jit(solution)/shard_map/all_to_all | solution.py:47
  164.3 0.0 copy-start.9
  164.3 0.0 copy-start.8
  164.3 4.9 %all-to-all-start.1 = ((bf16[32,112,768]{2,1,0:T(8,128)(2,1)}), bf16[32,112,768]{2,1,0:T(8,128)(2,1)}, u32[]{:S(2)}, u32[]{:S(2)}) async-start(bf16[32,112,768]{2,1,0:T(8,128)(2,1)} %get-tuple-element.22), calls=%async_computation.1 | async-start | bytes 11010048 | tf_op jit(solution)/shard_map/all_to_all | solution.py:47
  169.2 0.0 copy-done.9
  169.3 0.9 table_of.1.table_ref
  170.1 0.0 copy-done.8
  170.2 0.0 copy-start.4
  170.2 0.7 query_side.1
  170.9 0.0 copy-start.7
  170.9 0.8 copy-done.7
  171.7 0.0 copy-start
  171.7 0.0 copy-start.2
  171.7 2.0 summed_0.1.refs_0_
  173.7 0.0 copy-done.4
  173.8 0.0 copy-done
  173.8 0.5 copy-done.2
  174.3 4.1 %combine_0.1.refs_3_ = f32[384,1280]{1,0:T(8,128)S(1)} custom-call(bf16[384,1536]{1,0:T(8,128)(2,1)S(1)} %table_of.1.table_ref, bf16[384,1280]{1,0:T(8,128)(2,1)S(1)} %copy-done.4, bf16[1280,640]{1,0:T(8,128)(2,1)S(1)} %bitcast.20, bf16[1280,640]{1,0:T(8,128)(2,1)S(1)} %bitcast.24, bf16[32,112,512]{2,1,0:T(8,128)(2,1)} %all-to-all-done.2.refs_0_.refs_1_.refs_2_.back_ref, ...), custom_call_target="tpu_custom_call" | custom-call | flops 1107296256 | bytes 3866624 | tf_op jit(solution)/shard_map/combine_0/pallas_call | solution.py:326
  178.4 74.4 %all-to-all-done.1.refs_0_.refs_1_.refs_2_.back_ref = bf16[32,112,768]{2,1,0:T(8,128)(2,1)} async-done(((bf16[32,112,768]{2,1,0:T(8,128)(2,1)}), bf16[32,112,768]{2,1,0:T(8,128)(2,1)}, u32[]{:S(2)}, u32[]{:S(2)}) %all-to-all-start.1) | async-done | bytes 5505056 | tf_op jit(solution)/shard_map/all_to_all | solution.py:47
  252.8 0.0 copy-start.1
  252.8 0.0 copy-start.3
  252.8 0.0 copy-start.5
  252.9 1.1 collective-permute-start.1
  253.9 3.2 %summed_2.1 = f32[40,1920]{1,0:T(8,128)} custom-call(bf16[32,112,768]{2,1,0:T(8,128)(2,1)} %all-to-all-done.1.refs_0_.refs_1_.refs_2_.back_ref, f32[64,512]{1,0:T(8,128)S(1)} %summed_0.1.refs_0_), custom_call_target="tpu_custom_call" | custom-call | flops 1572864 | bytes 3145728 | tf_op jit(solution)/shard_map/summed_2/pallas_call | solution.py:380
  257.1 0.0 copy-done.1
  257.1 0.0 copy-done.3
  257.1 0.0 copy-done.5
  257.1 6.8 %combine_2.1 = bf16[384,1280]{1,0:T(8,128)(2,1)} custom-call(bf16[384,1536]{1,0:T(8,128)(2,1)S(1)} %table_of.1.table_ref, bf16[384,1280]{1,0:T(8,128)(2,1)S(1)} %copy-done.5, bf16[1280,640]{1,0:T(8,128)(2,1)S(1)} %bitcast.21, bf16[1280,640]{1,0:T(8,128)(2,1)S(1)} %bitcast.25, bf16[32,112,768]{2,1,0:T(8,128)(2,1)} %all-to-all-done.1.refs_0_.refs_1_.refs_2_.back_ref, ...), custom_call_target="tpu_custom_call" | custom-call | flops 1660944384 | bytes 5308416 | tf_op jit(solution)/shard_map/combine_2/pallas_call | solution.py:326
  263.9 0.0 collective-permute-done.1
  263.9 0.8 copy.18
Async XLA Ops:
  6.5 9.8 %copy-start.10 = (bf16[1,1,256,1280]{3,2,1,0:T(8,128)(2,1)S(1)}, bf16[1,1,256,1280]{3,2,1,0:T(8,128)(2,1)}, u32[]{:S(2)}) copy-start(bf16[1,1,256,1280]{3,2,1,0:T(8,128)(2,1)} %param.9) | copy-start | bytes 1966084
  6.5 48.7 %copy-start.6 = (bf16[1,1280,640]{2,1,0:T(8,128)(2,1)S(1)}, bf16[1,1280,640]{2,1,0:T(8,128)(2,1)}, u32[]{:S(2)}) copy-start(bf16[1,1280,640]{2,1,0:T(8,128)(2,1)} %param.10) | copy-start | bytes 4915204
  6.5 70.3 %all-to-all-start = ((bf16[32,48,1408]{2,1,0:T(8,128)(2,1)}), bf16[32,48,1408]{2,1,0:T(8,128)(2,1)}, u32[]{:S(2)}, u32[]{:S(2)}) async-start(bf16[32,48,1408]{2,1,0:T(8,128)(2,1)} %bitcast.29), calls=%async_computation | async-start | bytes 8650752 | tf_op jit(solution)/shard_map/all_to_all | solution.py:47
  16.4 38.8 %collective-permute-start = (bf16[256,1280]{1,0:T(8,128)(2,1)S(1)}, bf16[256,1280]{1,0:T(8,128)(2,1)S(1)}, u32[]{:S(2)}, u32[]{:S(2)}) collective-permute-start(bf16[256,1280]{1,0:T(8,128)(2,1)S(1)} %bitcast.36), channel_id=1, source_target_pairs={{0,1},{1,2},{2,3},{3,0},{4,5},{5,6},{6,7},{7,4},{8,9},{9,10},{10,1... | collective-permute-start | bytes 1966088 | tf_op jit(solution)/shard_map/ppermute | solution.py:43
  55.2 21.6 %copy-start.11 = (bf16[256,1280]{1,0:T(8,128)(2,1)}, bf16[256,1280]{1,0:T(8,128)(2,1)S(1)}, u32[]{:S(2)}) copy-start(bf16[256,1280]{1,0:T(8,128)(2,1)S(1)} %collective-permute-done.refs_6_) | copy-start | bytes 1966084
  96.0 68.3 %all-to-all-start.2 = ((bf16[32,112,512]{2,1,0:T(8,128)(2,1)}), bf16[32,112,512]{2,1,0:T(8,128)(2,1)}, u32[]{:S(2)}, u32[]{:S(2)}) async-start(bf16[32,112,512]{2,1,0:T(8,128)(2,1)} %get-tuple-element.24), calls=%async_computation.2 | async-start | bytes 7340032 | tf_op jit(solution)/shard_map/all_to_all | solution.py:47
  164.3 5.0 %copy-start.9 = (s32[1,1,384,2]{2,3,1,0:T(2,128)S(1)}, s32[1,1,384,2]{2,3,1,0:T(2,128)}, u32[]{:S(2)}) copy-start(s32[1,1,384,2]{2,3,1,0:T(2,128)} %param.8) | copy-start | bytes 9220
  164.3 5.9 %copy-start.8 = (bf16[256,640]{1,0:T(8,128)(2,1)S(1)}, bf16[256,640]{1,0:T(8,128)(2,1)}, u32[]{:S(2)}) copy-start(bf16[256,640]{1,0:T(8,128)(2,1)} %get-tuple-element.25.dq_ref) | copy-start | bytes 983044
  164.3 88.5 %all-to-all-start.1 = ((bf16[32,112,768]{2,1,0:T(8,128)(2,1)}), bf16[32,112,768]{2,1,0:T(8,128)(2,1)}, u32[]{:S(2)}, u32[]{:S(2)}) async-start(bf16[32,112,768]{2,1,0:T(8,128)(2,1)} %get-tuple-element.22), calls=%async_computation.1 | async-start | bytes 11010048 | tf_op jit(solution)/shard_map/all_to_all | solution.py:47
  170.2 3.6 %copy-start.4 = (bf16[384,1280]{1,0:T(8,128)(2,1)S(1)}, bf16[384,1280]{1,0:T(8,128)(2,1)}, u32[]{:S(2)}) copy-start(bf16[384,1280]{1,0:T(8,128)(2,1)} %get-tuple-element.28.down_ref) | copy-start | bytes 2949124
  170.9 0.8 copy-start.7
  171.7 2.1 copy-start
  171.7 2.6 copy-start.2
  252.8 4.3 %copy-start.1 = (bf16[1,1280,640]{2,1,0:T(8,128)(2,1)S(1)}, bf16[1,1280,640]{2,1,0:T(8,128)(2,1)}, u32[]{:S(2)}) copy-start(bf16[1,1280,640]{2,1,0:T(8,128)(2,1)} %param.11) | copy-start | bytes 4915204
  252.8 4.3 %copy-start.3 = (bf16[1,1280,640]{2,1,0:T(8,128)(2,1)S(1)}, bf16[1,1280,640]{2,1,0:T(8,128)(2,1)}, u32[]{:S(2)}) copy-start(bf16[1,1280,640]{2,1,0:T(8,128)(2,1)} %param.12) | copy-start | bytes 4915204
  252.8 4.3 %copy-start.5 = (bf16[384,1280]{1,0:T(8,128)(2,1)S(1)}, bf16[384,1280]{1,0:T(8,128)(2,1)}, u32[]{:S(2)}) copy-start(bf16[384,1280]{1,0:T(8,128)(2,1)} %get-tuple-element.28.down_ref) | copy-start | bytes 2949124
  252.9 11.1 %collective-permute-start.1 = (bf16[256,1280]{1,0:T(8,128)(2,1)}, bf16[256,1280]{1,0:T(8,128)(2,1)S(1)}, u32[]{:S(2)}, u32[]{:S(2)}) collective-permute-start(bf16[256,1280]{1,0:T(8,128)(2,1)} %copy-done.7), channel_id=1, source_target_pairs={{0,3},{1,0},{2,1},{3,2},{4,7},{5,4},{6,5},{7,6},{8,11},{9,8},{10,9... | collective-permute-start | bytes 1966088 | tf_op jit(solution)/shard_map/ppermute | solution.py:43

commit v5 on v4

--- a/solution.py
+++ b/solution.py
@@ -406,6 +406,7 @@
 
     entering = passed_along(hidden[0, 0], "section", 1)
     out = dispatch(capacity, readers, dest.T, own)
+    out, entering = lax.optimization_barrier((out, entering))
     queries = jnp.dot(entering, wq, preferred_element_type=F32).astype(BF16)
     got = exchanged(out.reshape(readers, capacity, -1)).reshape(slots, -1)
 

time: 268 us -> 254 us (0.948); the launches traced: 265 us -> 254 us
  starting transfers between devices: 33.3 us -> 27.3 us
  waiting for transfers between devices: 158 us -> 154 us
    ppermute x2, waiting for transfers between devices: 36.6 us -> 1.98 us  [passed_along(): return lax.ppermute(value, axis, pairs)]
    all_to_all x3, waiting for transfers between devices: 122 us -> 152 us  [exchanged(): return lax.all_to_all(value, 'dp', split_axis=0, concat_axis=0, tiled=True)]
    all_to_all x3, starting transfers between devices: 30 us -> 24.7 us  [exchanged(): return lax.all_to_all(value, 'dp', split_axis=0, concat_axis=0, tiled=True)]
  transfers between devices with their start and end apart: 5 -> 5, of which waited for: 4 -> 4; matrix products, arithmetic and copies ran while one was open for 1% -> 1% of each run, Pallas kernels for 17% -> 19%
where the time goes in v5:
time: 254 us
  waiting for transfers between devices  154 us (61%)
  Pallas kernels  68.6 us (27%)
  starting transfers between devices  27.3 us (11%)
    all_to_all x3, waiting for transfers between devices, exchanged(): return lax.all_to_all(value, 'dp', split_axis=0, concat_axis=0, tiled=True)  152 us
    pallas_call x2, Pallas kernels, attend(): pl.pallas_call(functools.partial(attend_kernel, len(filled)), grid=(pairs...  45.3 us
    all_to_all x3, starting transfers between devices, exchanged(): return lax.all_to_all(value, 'dp', split_axis=0, concat_axis=0, tiled=True)  24.7 us
    pallas_call x2, Pallas kernels, combine(): pl.pallas_call(functools.partial(combine_kernel, len(held)), grid=(pairs,...  10.9 us
    pallas_call x1, Pallas kernels, dispatch(): pl.pallas_call(functools.partial(dispatch_kernel, capacity), grid=(slots...  5.87 us
  transfers between devices with their start and end apart: 5, of which 4 were waited for; matrix products, arithmetic and copies ran while one was open for 1% of the time, Pallas kernels for 19%

profile of v5, /device:TPU:11, one launch (start us, length us, event | category | flops | bytes accessed | tf_op | source)
XLA Modules:
  0.0 254.0 jit_solution(18019590252718385110)
XLA Ops:
  0.6 0.8 collective-permute-start
  1.4 5.9 %dispatch.1 = bf16[1536,1408]{1,0:T(8,128)(2,1)} custom-call(s32[2,384]{1,0:T(2,128)} %bitcast.27, bf16[384,1280]{1,0:T(8,128)(2,1)} %bitcast.33), custom_call_target="tpu_custom_call" | custom-call | flops 1509949440 | bytes 4915200 | tf_op jit(solution)/shard_map/dispatch/pallas_call | solution.py:109
  7.3 2.0 collective-permute-done.refs_6_
  9.3 0.0 copy-start.10
  9.3 0.0 copy-start.6
  9.3 10.1 %all-to-all-start = ((bf16[32,48,1408]{2,1,0:T(8,128)(2,1)}), bf16[32,48,1408]{2,1,0:T(8,128)(2,1)}, u32[]{:S(2)}, u32[]{:S(2)}) async-start(bf16[32,48,1408]{2,1,0:T(8,128)(2,1)} %bitcast.29), calls=%async_computation | async-start | bytes 8650752 | tf_op jit(solution)/shard_map/all_to_all | solution.py:47
  19.4 0.0 copy-done.10
  19.4 0.0 copy-done.6
  19.4 1.4 convolution_convert_fusion.refs_0_
  20.8 59.8 %all-to-all-done = bf16[32,48,1408]{2,1,0:T(8,128)(2,1)} async-done(((bf16[32,48,1408]{2,1,0:T(8,128)(2,1)}), bf16[32,48,1408]{2,1,0:T(8,128)(2,1)}, u32[]{:S(2)}, u32[]{:S(2)}) %all-to-all-start) | async-done | bytes 4325408 | tf_op jit(solution)/shard_map/all_to_all | solution.py:47
  80.6 19.2 %attend_0.1 = (bf16[256,640]{1,0:T(8,128)(2,1)}, bf16[256,640]{1,0:T(8,128)(2,1)}, bf16[384,1280]{1,0:T(8,128)(2,1)}, bf16[32,112,512]{2,1,0:T(8,128)(2,1)}) custom-call(bf16[256,640]{1,0:T(8,128)(2,1)} %convolution_convert_fusion.refs_0_, bf16[256,640]{1,0:T(8,128)(2,1)} %bitcast.37, bf16[384,1280]{1,0:T(8,128)(2,1)} %bitcast.34, ...), custom_call_target="tpu_custom_call" | custom-call | flops 11072962560 | bytes 10813440 | tf_op jit(solution)/shard_map/attend_0/pallas_call | solution.py:215
  99.8 5.4 %all-to-all-start.2 = ((bf16[32,112,512]{2,1,0:T(8,128)(2,1)}), bf16[32,112,512]{2,1,0:T(8,128)(2,1)}, u32[]{:S(2)}, u32[]{:S(2)}) async-start(bf16[32,112,512]{2,1,0:T(8,128)(2,1)} %get-tuple-element.28), calls=%async_computation.2 | async-start | bytes 7340032 | tf_op jit(solution)/shard_map/all_to_all | solution.py:47
  105.2 26.0 %attend_2.1 = (bf16[256,640]{1,0:T(8,128)(2,1)}, bf16[256,640]{1,0:T(8,128)(2,1)}, bf16[384,1280]{1,0:T(8,128)(2,1)}, bf16[32,112,768]{2,1,0:T(8,128)(2,1)}) custom-call(bf16[256,640]{1,0:T(8,128)(2,1)} %convolution_convert_fusion.refs_0_, bf16[256,640]{1,0:T(8,128)(2,1)} %bitcast.38, ...), custom_call_target="tpu_custom_call", output_to_operand_aliasing={{0}: (7, {}), {1}: (8, {}), {2}: (9, {})} | custom-call | flops 16609443840 | bytes 13762560 | tf_op jit(solution)/shard_map/attend_2/pallas_call | solution.py:215
  131.2 20.8 %all-to-all-done.2.refs_0_.refs_1_.refs_2_.back_ref = bf16[32,112,512]{2,1,0:T(8,128)(2,1)} async-done(((bf16[32,112,512]{2,1,0:T(8,128)(2,1)}), bf16[32,112,512]{2,1,0:T(8,128)(2,1)}, u32[]{:S(2)}, u32[]{:S(2)}) %all-to-all-start.2) | async-done | bytes 3670048 | tf_op jit(solution)/shard_map/all_to_all | solution.py:47
  152.1 0.0 copy-start.9
  152.1 0.0 copy-start.8
  152.1 9.2 %all-to-all-start.1 = ((bf16[32,112,768]{2,1,0:T(8,128)(2,1)}), bf16[32,112,768]{2,1,0:T(8,128)(2,1)}, u32[]{:S(2)}, u32[]{:S(2)}) async-start(bf16[32,112,768]{2,1,0:T(8,128)(2,1)} %get-tuple-element.26), calls=%async_computation.1 | async-start | bytes 11010048 | tf_op jit(solution)/shard_map/all_to_all | solution.py:47
  161.3 0.0 copy-done.9
  161.3 0.9 table_of.1.table_ref
  162.2 0.0 copy-done.8
  162.2 0.0 copy-start.4
  162.2 0.7 query_side.1
  163.0 0.0 copy-start.7
  163.0 0.8 copy-done.7
  163.8 0.0 copy-start
  163.8 0.0 copy-start.2
  163.8 2.0 summed_0.1.refs_0_
  165.8 0.0 copy-done.4
  165.8 0.0 copy-done
  165.9 0.5 copy-done.2
  166.3 4.1 %combine_0.1.refs_3_ = f32[384,1280]{1,0:T(8,128)S(1)} custom-call(bf16[384,1536]{1,0:T(8,128)(2,1)S(1)} %table_of.1.table_ref, bf16[384,1280]{1,0:T(8,128)(2,1)S(1)} %copy-done.4, bf16[1280,640]{1,0:T(8,128)(2,1)S(1)} %bitcast.20, bf16[1280,640]{1,0:T(8,128)(2,1)S(1)} %bitcast.24, bf16[32,112,512]{2,1,0:T(8,128)(2,1)} %all-to-all-done.2.refs_0_.refs_1_.refs_2_.back_ref, ...), custom_call_target="tpu_custom_call" | custom-call | flops 1107296256 | bytes 3866624 | tf_op jit(solution)/shard_map/combine_0/pallas_call | solution.py:326
  170.5 71.1 %all-to-all-done.1.refs_0_.refs_1_.refs_2_.back_ref = bf16[32,112,768]{2,1,0:T(8,128)(2,1)} async-done(((bf16[32,112,768]{2,1,0:T(8,128)(2,1)}), bf16[32,112,768]{2,1,0:T(8,128)(2,1)}, u32[]{:S(2)}, u32[]{:S(2)}) %all-to-all-start.1) | async-done | bytes 5505056 | tf_op jit(solution)/shard_map/all_to_all | solution.py:47
  241.6 0.0 copy-start.1
  241.6 0.0 copy-start.3
  241.6 0.0 copy-start.5
  241.6 1.8 collective-permute-start.1
  243.4 3.0 %summed_2.1 = f32[40,1920]{1,0:T(8,128)} custom-call(bf16[32,112,768]{2,1,0:T(8,128)(2,1)} %all-to-all-done.1.refs_0_.refs_1_.refs_2_.back_ref, f32[64,512]{1,0:T(8,128)S(1)} %summed_0.1.refs_0_), custom_call_target="tpu_custom_call" | custom-call | flops 1572864 | bytes 3145728 | tf_op jit(solution)/shard_map/summed_2/pallas_call | solution.py:380
  246.4 0.0 copy-done.1
  246.4 0.0 copy-done.3
  246.4 0.0 copy-done.5
  246.4 6.8 %combine_2.1 = bf16[384,1280]{1,0:T(8,128)(2,1)} custom-call(bf16[384,1536]{1,0:T(8,128)(2,1)S(1)} %table_of.1.table_ref, bf16[384,1280]{1,0:T(8,128)(2,1)S(1)} %copy-done.5, bf16[1280,640]{1,0:T(8,128)(2,1)S(1)} %bitcast.21, bf16[1280,640]{1,0:T(8,128)(2,1)S(1)} %bitcast.25, bf16[32,112,768]{2,1,0:T(8,128)(2,1)} %all-to-all-done.1.refs_0_.refs_1_.refs_2_.back_ref, ...), custom_call_target="tpu_custom_call" | custom-call | flops 1660944384 | bytes 5308416 | tf_op jit(solution)/shard_map/combine_2/pallas_call | solution.py:326
  253.2 0.0 collective-permute-done.1
  253.2 0.8 copy.18
Async XLA Ops:
  0.6 8.6 %collective-permute-start = (bf16[256,1280]{1,0:T(8,128)(2,1)}, bf16[256,1280]{1,0:T(8,128)(2,1)S(1)}, u32[]{:S(2)}, u32[]{:S(2)}) collective-permute-start(bf16[256,1280]{1,0:T(8,128)(2,1)} %bitcast.36), channel_id=1, source_target_pairs={{0,1},{1,2},{2,3},{3,0},{4,5},{5,6},{6,7},{7,4},{8,9},{9,10},{10,1... | collective-permute-start | bytes 1966088 | tf_op jit(solution)/shard_map/ppermute | solution.py:43
  9.3 10.1 %copy-start.10 = (bf16[256,1280]{1,0:T(8,128)(2,1)}, bf16[256,1280]{1,0:T(8,128)(2,1)S(1)}, u32[]{:S(2)}) copy-start(bf16[256,1280]{1,0:T(8,128)(2,1)S(1)} %collective-permute-done.refs_6_) | copy-start | bytes 1966084
  9.3 10.1 %copy-start.6 = (bf16[1,1280,640]{2,1,0:T(8,128)(2,1)S(1)}, bf16[1,1280,640]{2,1,0:T(8,128)(2,1)}, u32[]{:S(2)}) copy-start(bf16[1,1280,640]{2,1,0:T(8,128)(2,1)} %param.10) | copy-start | bytes 4915204
  9.3 71.3 %all-to-all-start = ((bf16[32,48,1408]{2,1,0:T(8,128)(2,1)}), bf16[32,48,1408]{2,1,0:T(8,128)(2,1)}, u32[]{:S(2)}, u32[]{:S(2)}) async-start(bf16[32,48,1408]{2,1,0:T(8,128)(2,1)} %bitcast.29), calls=%async_computation | async-start | bytes 8650752 | tf_op jit(solution)/shard_map/all_to_all | solution.py:47
  99.8 52.2 %all-to-all-start.2 = ((bf16[32,112,512]{2,1,0:T(8,128)(2,1)}), bf16[32,112,512]{2,1,0:T(8,128)(2,1)}, u32[]{:S(2)}, u32[]{:S(2)}) async-start(bf16[32,112,512]{2,1,0:T(8,128)(2,1)} %get-tuple-element.28), calls=%async_computation.2 | async-start | bytes 7340032 | tf_op jit(solution)/shard_map/all_to_all | solution.py:47
  152.1 9.2 %copy-start.9 = (s32[1,1,384,2]{2,3,1,0:T(2,128)S(1)}, s32[1,1,384,2]{2,3,1,0:T(2,128)}, u32[]{:S(2)}) copy-start(s32[1,1,384,2]{2,3,1,0:T(2,128)} %param.8) | copy-start | bytes 9220
  152.1 10.1 %copy-start.8 = (bf16[256,640]{1,0:T(8,128)(2,1)S(1)}, bf16[256,640]{1,0:T(8,128)(2,1)}, u32[]{:S(2)}) copy-start(bf16[256,640]{1,0:T(8,128)(2,1)} %get-tuple-element.29.dq_ref) | copy-start | bytes 983044
  152.1 89.5 %all-to-all-start.1 = ((bf16[32,112,768]{2,1,0:T(8,128)(2,1)}), bf16[32,112,768]{2,1,0:T(8,128)(2,1)}, u32[]{:S(2)}, u32[]{:S(2)}) async-start(bf16[32,112,768]{2,1,0:T(8,128)(2,1)} %get-tuple-element.26), calls=%async_computation.1 | async-start | bytes 11010048 | tf_op jit(solution)/shard_map/all_to_all | solution.py:47
  162.2 3.6 %copy-start.4 = (bf16[384,1280]{1,0:T(8,128)(2,1)S(1)}, bf16[384,1280]{1,0:T(8,128)(2,1)}, u32[]{:S(2)}) copy-start(bf16[384,1280]{1,0:T(8,128)(2,1)} %get-tuple-element.32.down_ref) | copy-start | bytes 2949124
  163.0 0.8 copy-start.7
  163.8 2.1 copy-start
  163.8 2.6 %copy-start.2 = (bf16[1,1280,640]{2,1,0:T(8,128)(2,1)S(1)}, bf16[1,1280,640]{2,1,0:T(8,128)(2,1)}, u32[]{:S(2)}) copy-start(bf16[1,1280,640]{2,1,0:T(8,128)(2,1)} %param.12) | copy-start | bytes 4915204
  241.6 4.8 %copy-start.1 = (bf16[1,1280,640]{2,1,0:T(8,128)(2,1)S(1)}, bf16[1,1280,640]{2,1,0:T(8,128)(2,1)}, u32[]{:S(2)}) copy-start(bf16[1,1280,640]{2,1,0:T(8,128)(2,1)} %param.11) | copy-start | bytes 4915204
  241.6 4.8 %copy-start.3 = (bf16[1,1280,640]{2,1,0:T(8,128)(2,1)S(1)}, bf16[1,1280,640]{2,1,0:T(8,128)(2,1)}, u32[]{:S(2)}) copy-start(bf16[1,1280,640]{2,1,0:T(8,128)(2,1)} %param.12) | copy-start | bytes 4915204
  241.6 4.8 %copy-start.5 = (bf16[384,1280]{1,0:T(8,128)(2,1)S(1)}, bf16[384,1280]{1,0:T(8,128)(2,1)}, u32[]{:S(2)}) copy-start(bf16[384,1280]{1,0:T(8,128)(2,1)} %get-tuple-element.32.down_ref) | copy-start | bytes 2949124
  241.6 11.6 %collective-permute-start.1 = (bf16[256,1280]{1,0:T(8,128)(2,1)}, bf16[256,1280]{1,0:T(8,128)(2,1)S(1)}, u32[]{:S(2)}, u32[]{:S(2)}) collective-permute-start(bf16[256,1280]{1,0:T(8,128)(2,1)} %copy-done.7), channel_id=1, source_target_pairs={{0,3},{1,0},{2,1},{3,2},{4,7},{5,4},{6,5},{7,6},{8,11},{9,8},{10,9... | collective-permute-start | bytes 1966088 | tf_op jit(solution)/shard_map/ppermute | solution.py:43

commit v6 on v5

--- a/solution.py
+++ b/solution.py
@@ -346,7 +346,7 @@
     )(table, down, wk, wv, *([back] * (SLOTS // STEP)), *held)
 
 
-def sum_kernel(last, back_ref, *refs):
+def sum_kernel(first, last, back_ref, *refs):
     held, out_ref = refs[:-1], refs[-1]
 
     def added(lanes):
@@ -355,36 +355,43 @@
             sums[a % 4] = sums[a % 4] + back_ref[a, :, lanes].astype(F32)
         return (sums[0] + sums[1]) + (sums[2] + sums[3])
 
-    mine = [added(slice(c, c + PAIR)) for c in range(0, back_ref.shape[2], PAIR)]
+    upper, lower = added(slice(0, PAIR)), added(slice(PAIR, 2 * PAIR))
     if not last:
-        out_ref[...] = jnp.concatenate(mine, axis=1)
+        out_ref[...] = jnp.concatenate([upper, lower], axis=1)
         return
-    pieces = []
-    for r in held:
-        pieces += [r[:, c : c + PAIR] for c in range(0, r.shape[1], PAIR)]
-    pieces += mine
     heads = out_ref.shape[1] // 3
-    for p in range(heads // PAIR):
-        upper, lower = pieces[2 * p], pieces[2 * p + 1]
-        at = slice(p * PAIR, (p + 1) * PAIR)
-        out_ref[:TWICE, at] = upper[ROWS:]
-        out_ref[TWICE:, at] = lower[2 * TWICE :]
-        out_ref[:, heads + p * PAIR : heads + (p + 1) * PAIR] = upper[:ROWS]
-        out_ref[:, 2 * heads + p * PAIR : 2 * heads + (p + 1) * PAIR] = lower[:ROWS]
+
+    def place(pair, upper, lower):
+        at = [pl.ds(pl.multiple_of(part * heads + pair * PAIR, PAIR), PAIR) for part in range(3)]
+        out_ref[:TWICE, at[0]] = upper[ROWS:]
+        out_ref[TWICE:, at[0]] = lower[2 * TWICE :]
+        out_ref[:, at[1]] = upper[:ROWS]
+        out_ref[:, at[2]] = lower[:ROWS]
+
+    place(first + pl.program_id(0), upper, lower)
+
+    @pl.when(pl.program_id(0) == 0)
+    def _():
+        pair = 0
+        for r in held:
+            for c in range(0, r.shape[1], 2 * PAIR):
+                place(pair, r[:, c : c + PAIR], r[:, c + PAIR : c + 2 * PAIR])
+                pair += 1
 
 
 def summed(first, last, heads, back, held):
     readers, _, lanes = back.shape
     shape = (ROWS, 3 * heads) if last else (GRADS, lanes)
-    whole = lambda i: (0, 0)
-    return pl.pallas_call(
-        functools.partial(sum_kernel, last),
-        grid=(1,),
-        in_specs=[pl.BlockSpec((readers, GRADS, lanes), lambda i: (0, 0, 0))]
+    whole = lambda p: (0, 0)
+    here = pl.BlockSpec((GRADS, 2 * PAIR), lambda p: (0, p))
+    return pl.pallas_call(
+        functools.partial(sum_kernel, first, last),
+        grid=(lanes // (2 * PAIR),),
+        in_specs=[pl.BlockSpec((readers, GRADS, 2 * PAIR), lambda p: (0, 0, p))]
         + [pl.BlockSpec(h.shape, whole) for h in held],
-        out_specs=pl.BlockSpec(shape, whole),
+        out_specs=pl.BlockSpec(shape, whole) if last else here,
         out_shape=jax.ShapeDtypeStruct(shape, F32),
-        compiler_params=params(SMALL),
+        compiler_params=params(SMALL, dimension_semantics=("arbitrary",)),
         cost_estimate=cost(readers * GRADS * lanes, 2 * readers * GRADS * lanes),
         name=f"summed_{first}",
     )(back, *held)

time: 254 us -> 255 us (level)
  transfers between devices with their start and end apart: 5 -> 5, of which waited for: 4 -> 4; matrix products, arithmetic and copies ran while one was open for 1% -> 1% of each run, Pallas kernels for 19% -> 20%
where the time goes in v6:
time: 255 us
  waiting for transfers between devices  154 us (60%)
  Pallas kernels  69.1 us (27%)
  starting transfers between devices  27.3 us (11%)
    all_to_all x3, waiting for transfers between devices, exchanged(): return lax.all_to_all(value, 'dp', split_axis=0, concat_axis=0, tiled=True)  152 us
    pallas_call x2, Pallas kernels, attend(): pl.pallas_call(functools.partial(attend_kernel, len(filled)), grid=(pairs...  45.3 us
    all_to_all x3, starting transfers between devices, exchanged(): return lax.all_to_all(value, 'dp', split_axis=0, concat_axis=0, tiled=True)  24.7 us
    pallas_call x2, Pallas kernels, combine(): pl.pallas_call(functools.partial(combine_kernel, len(held)), grid=(pairs,...  10.9 us
    pallas_call x1, Pallas kernels, dispatch(): pl.pallas_call(functools.partial(dispatch_kernel, capacity), grid=(slots...  5.87 us
    pallas_call x2, Pallas kernels, summed(): pl.pallas_call(functools.partial(sum_kernel, first, last), grid=(lanes //...  5.47 us
  transfers between devices with their start and end apart: 5, of which 4 were waited for; matrix products, arithmetic and copies ran while one was open for 1% of the time, Pallas kernels for 20%

profile of v6, /device:TPU:11, one launch (start us, length us, event | category | flops | bytes accessed | tf_op | source)
XLA Modules:
  0.0 254.6 jit_solution(13566527315650510848)
XLA Ops:
  0.6 0.8 collective-permute-start
  1.4 5.9 %dispatch.1 = bf16[1536,1408]{1,0:T(8,128)(2,1)} custom-call(s32[2,384]{1,0:T(2,128)} %bitcast.27, bf16[384,1280]{1,0:T(8,128)(2,1)} %bitcast.33), custom_call_target="tpu_custom_call" | custom-call | flops 1509949440 | bytes 4915200 | tf_op jit(solution)/shard_map/dispatch/pallas_call | solution.py:109
  7.3 2.0 collective-permute-done.refs_6_
  9.3 0.0 copy-start.10
  9.3 0.0 copy-start.6
  9.3 10.1 %all-to-all-start = ((bf16[32,48,1408]{2,1,0:T(8,128)(2,1)}), bf16[32,48,1408]{2,1,0:T(8,128)(2,1)}, u32[]{:S(2)}, u32[]{:S(2)}) async-start(bf16[32,48,1408]{2,1,0:T(8,128)(2,1)} %bitcast.29), calls=%async_computation | async-start | bytes 8650752 | tf_op jit(solution)/shard_map/all_to_all | solution.py:47
  19.4 0.0 copy-done.10
  19.4 0.0 copy-done.6
  19.4 1.4 convolution_convert_fusion.refs_0_
  20.8 59.8 %all-to-all-done = bf16[32,48,1408]{2,1,0:T(8,128)(2,1)} async-done(((bf16[32,48,1408]{2,1,0:T(8,128)(2,1)}), bf16[32,48,1408]{2,1,0:T(8,128)(2,1)}, u32[]{:S(2)}, u32[]{:S(2)}) %all-to-all-start) | async-done | bytes 4325408 | tf_op jit(solution)/shard_map/all_to_all | solution.py:47
  80.6 19.2 %attend_0.1 = (bf16[256,640]{1,0:T(8,128)(2,1)}, bf16[256,640]{1,0:T(8,128)(2,1)}, bf16[384,1280]{1,0:T(8,128)(2,1)}, bf16[32,112,512]{2,1,0:T(8,128)(2,1)}) custom-call(bf16[256,640]{1,0:T(8,128)(2,1)} %convolution_convert_fusion.refs_0_, bf16[256,640]{1,0:T(8,128)(2,1)} %bitcast.37, bf16[384,1280]{1,0:T(8,128)(2,1)} %bitcast.34, ...), custom_call_target="tpu_custom_call" | custom-call | flops 11072962560 | bytes 10813440 | tf_op jit(solution)/shard_map/attend_0/pallas_call | solution.py:215
  99.8 5.4 %all-to-all-start.2 = ((bf16[32,112,512]{2,1,0:T(8,128)(2,1)}), bf16[32,112,512]{2,1,0:T(8,128)(2,1)}, u32[]{:S(2)}, u32[]{:S(2)}) async-start(bf16[32,112,512]{2,1,0:T(8,128)(2,1)} %get-tuple-element.28), calls=%async_computation.2 | async-start | bytes 7340032 | tf_op jit(solution)/shard_map/all_to_all | solution.py:47
  105.2 26.0 %attend_2.1 = (bf16[256,640]{1,0:T(8,128)(2,1)}, bf16[256,640]{1,0:T(8,128)(2,1)}, bf16[384,1280]{1,0:T(8,128)(2,1)}, bf16[32,112,768]{2,1,0:T(8,128)(2,1)}) custom-call(bf16[256,640]{1,0:T(8,128)(2,1)} %convolution_convert_fusion.refs_0_, bf16[256,640]{1,0:T(8,128)(2,1)} %bitcast.38, ...), custom_call_target="tpu_custom_call", output_to_operand_aliasing={{0}: (7, {}), {1}: (8, {}), {2}: (9, {})} | custom-call | flops 16609443840 | bytes 13762560 | tf_op jit(solution)/shard_map/attend_2/pallas_call | solution.py:215
  131.2 20.8 %all-to-all-done.2.refs_0_.refs_1_.refs_2_.back_ref = bf16[32,112,512]{2,1,0:T(8,128)(2,1)} async-done(((bf16[32,112,512]{2,1,0:T(8,128)(2,1)}), bf16[32,112,512]{2,1,0:T(8,128)(2,1)}, u32[]{:S(2)}, u32[]{:S(2)}) %all-to-all-start.2) | async-done | bytes 3670048 | tf_op jit(solution)/shard_map/all_to_all | solution.py:47
  152.1 0.0 copy-start.9
  152.1 0.0 copy-start.8
  152.1 9.2 %all-to-all-start.1 = ((bf16[32,112,768]{2,1,0:T(8,128)(2,1)}), bf16[32,112,768]{2,1,0:T(8,128)(2,1)}, u32[]{:S(2)}, u32[]{:S(2)}) async-start(bf16[32,112,768]{2,1,0:T(8,128)(2,1)} %get-tuple-element.26), calls=%async_computation.1 | async-start | bytes 11010048 | tf_op jit(solution)/shard_map/all_to_all | solution.py:47
  161.3 0.0 copy-done.9
  161.3 0.9 table_of.1.table_ref
  162.2 0.0 copy-done.8
  162.2 0.0 copy-start.4
  162.2 0.7 query_side.1
  163.0 0.0 copy-start.7
  163.0 0.8 copy-done.7
  163.8 0.0 copy-start
  163.8 0.0 copy-start.2
  163.8 1.9 summed_0.1.refs_0_
  165.7 0.0 copy-done.4
  165.7 0.2 copy-done
  165.9 0.5 copy-done.2
  166.4 4.1 %combine_0.1.refs_3_ = f32[384,1280]{1,0:T(8,128)S(1)} custom-call(bf16[384,1536]{1,0:T(8,128)(2,1)S(1)} %table_of.1.table_ref, bf16[384,1280]{1,0:T(8,128)(2,1)S(1)} %copy-done.4, bf16[1280,640]{1,0:T(8,128)(2,1)S(1)} %bitcast.20, bf16[1280,640]{1,0:T(8,128)(2,1)S(1)} %bitcast.24, bf16[32,112,512]{2,1,0:T(8,128)(2,1)} %all-to-all-done.2.refs_0_.refs_1_.refs_2_.back_ref, ...), custom_call_target="tpu_custom_call" | custom-call | flops 1107296256 | bytes 3866624 | tf_op jit(solution)/shard_map/combine_0/pallas_call | solution.py:326
  170.5 71.1 %all-to-all-done.1.refs_0_.refs_1_.refs_2_.back_ref = bf16[32,112,768]{2,1,0:T(8,128)(2,1)} async-done(((bf16[32,112,768]{2,1,0:T(8,128)(2,1)}), bf16[32,112,768]{2,1,0:T(8,128)(2,1)}, u32[]{:S(2)}, u32[]{:S(2)}) %all-to-all-start.1) | async-done | bytes 5505056 | tf_op jit(solution)/shard_map/all_to_all | solution.py:47
  241.6 0.0 copy-start.1
  241.6 0.0 copy-start.3
  241.6 0.0 copy-start.5
  241.6 1.8 collective-permute-start.1
  243.4 3.6 %summed_2.1 = f32[40,1920]{1,0:T(8,128)} custom-call(bf16[32,112,768]{2,1,0:T(8,128)(2,1)} %all-to-all-done.1.refs_0_.refs_1_.refs_2_.back_ref, f32[64,512]{1,0:T(8,128)S(1)} %summed_0.1.refs_0_), custom_call_target="tpu_custom_call" | custom-call | flops 1572864 | bytes 3145728 | tf_op jit(solution)/shard_map/summed_2/pallas_call | solution.py:387
  247.0 0.0 copy-done.1
  247.0 0.0 copy-done.3
  247.0 0.0 copy-done.5
  247.0 6.8 %combine_2.1 = bf16[384,1280]{1,0:T(8,128)(2,1)} custom-call(bf16[384,1536]{1,0:T(8,128)(2,1)S(1)} %table_of.1.table_ref, bf16[384,1280]{1,0:T(8,128)(2,1)S(1)} %copy-done.5, bf16[1280,640]{1,0:T(8,128)(2,1)S(1)} %bitcast.21, bf16[1280,640]{1,0:T(8,128)(2,1)S(1)} %bitcast.25, bf16[32,112,768]{2,1,0:T(8,128)(2,1)} %all-to-all-done.1.refs_0_.refs_1_.refs_2_.back_ref, ...), custom_call_target="tpu_custom_call" | custom-call | flops 1660944384 | bytes 5308416 | tf_op jit(solution)/shard_map/combine_2/pallas_call | solution.py:326
  253.8 0.0 collective-permute-done.1
  253.8 0.8 copy.18
Async XLA Ops:
  0.6 8.6 %collective-permute-start = (bf16[256,1280]{1,0:T(8,128)(2,1)}, bf16[256,1280]{1,0:T(8,128)(2,1)S(1)}, u32[]{:S(2)}, u32[]{:S(2)}) collective-permute-start(bf16[256,1280]{1,0:T(8,128)(2,1)} %bitcast.36), channel_id=1, source_target_pairs={{0,1},{1,2},{2,3},{3,0},{4,5},{5,6},{6,7},{7,4},{8,9},{9,10},{10,1... | collective-permute-start | bytes 1966088 | tf_op jit(solution)/shard_map/ppermute | solution.py:43
  9.3 10.1 %copy-start.10 = (bf16[256,1280]{1,0:T(8,128)(2,1)}, bf16[256,1280]{1,0:T(8,128)(2,1)S(1)}, u32[]{:S(2)}) copy-start(bf16[256,1280]{1,0:T(8,128)(2,1)S(1)} %collective-permute-done.refs_6_) | copy-start | bytes 1966084
  9.3 10.1 %copy-start.6 = (bf16[1,1280,640]{2,1,0:T(8,128)(2,1)S(1)}, bf16[1,1280,640]{2,1,0:T(8,128)(2,1)}, u32[]{:S(2)}) copy-start(bf16[1,1280,640]{2,1,0:T(8,128)(2,1)} %param.10) | copy-start | bytes 4915204
  9.3 71.3 %all-to-all-start = ((bf16[32,48,1408]{2,1,0:T(8,128)(2,1)}), bf16[32,48,1408]{2,1,0:T(8,128)(2,1)}, u32[]{:S(2)}, u32[]{:S(2)}) async-start(bf16[32,48,1408]{2,1,0:T(8,128)(2,1)} %bitcast.29), calls=%async_computation | async-start | bytes 8650752 | tf_op jit(solution)/shard_map/all_to_all | solution.py:47
  99.8 52.2 %all-to-all-start.2 = ((bf16[32,112,512]{2,1,0:T(8,128)(2,1)}), bf16[32,112,512]{2,1,0:T(8,128)(2,1)}, u32[]{:S(2)}, u32[]{:S(2)}) async-start(bf16[32,112,512]{2,1,0:T(8,128)(2,1)} %get-tuple-element.28), calls=%async_computation.2 | async-start | bytes 7340032 | tf_op jit(solution)/shard_map/all_to_all | solution.py:47
  152.1 9.2 %copy-start.9 = (s32[1,1,384,2]{2,3,1,0:T(2,128)S(1)}, s32[1,1,384,2]{2,3,1,0:T(2,128)}, u32[]{:S(2)}) copy-start(s32[1,1,384,2]{2,3,1,0:T(2,128)} %param.8) | copy-start | bytes 9220
  152.1 10.1 %copy-start.8 = (bf16[256,640]{1,0:T(8,128)(2,1)S(1)}, bf16[256,640]{1,0:T(8,128)(2,1)}, u32[]{:S(2)}) copy-start(bf16[256,640]{1,0:T(8,128)(2,1)} %get-tuple-element.29.dq_ref) | copy-start | bytes 983044
  152.1 89.5 %all-to-all-start.1 = ((bf16[32,112,768]{2,1,0:T(8,128)(2,1)}), bf16[32,112,768]{2,1,0:T(8,128)(2,1)}, u32[]{:S(2)}, u32[]{:S(2)}) async-start(bf16[32,112,768]{2,1,0:T(8,128)(2,1)} %get-tuple-element.26), calls=%async_computation.1 | async-start | bytes 11010048 | tf_op jit(solution)/shard_map/all_to_all | solution.py:47
  162.2 3.5 %copy-start.4 = (bf16[384,1280]{1,0:T(8,128)(2,1)S(1)}, bf16[384,1280]{1,0:T(8,128)(2,1)}, u32[]{:S(2)}) copy-start(bf16[384,1280]{1,0:T(8,128)(2,1)} %get-tuple-element.32.down_ref) | copy-start | bytes 2949124
  163.0 0.8 copy-start.7
  163.8 2.1 copy-start
  163.8 2.6 %copy-start.2 = (bf16[1,1280,640]{2,1,0:T(8,128)(2,1)S(1)}, bf16[1,1280,640]{2,1,0:T(8,128)(2,1)}, u32[]{:S(2)}) copy-start(bf16[1,1280,640]{2,1,0:T(8,128)(2,1)} %param.12) | copy-start | bytes 4915204
  241.6 5.4 %copy-start.1 = (bf16[1,1280,640]{2,1,0:T(8,128)(2,1)S(1)}, bf16[1,1280,640]{2,1,0:T(8,128)(2,1)}, u32[]{:S(2)}) copy-start(bf16[1,1280,640]{2,1,0:T(8,128)(2,1)} %param.11) | copy-start | bytes 4915204
  241.6 5.4 %copy-start.3 = (bf16[1,1280,640]{2,1,0:T(8,128)(2,1)S(1)}, bf16[1,1280,640]{2,1,0:T(8,128)(2,1)}, u32[]{:S(2)}) copy-start(bf16[1,1280,640]{2,1,0:T(8,128)(2,1)} %param.12) | copy-start | bytes 4915204
  241.6 5.4 %copy-start.5 = (bf16[384,1280]{1,0:T(8,128)(2,1)S(1)}, bf16[384,1280]{1,0:T(8,128)(2,1)}, u32[]{:S(2)}) copy-start(bf16[384,1280]{1,0:T(8,128)(2,1)} %get-tuple-element.32.down_ref) | copy-start | bytes 2949124
  241.6 12.2 %collective-permute-start.1 = (bf16[256,1280]{1,0:T(8,128)(2,1)}, bf16[256,1280]{1,0:T(8,128)(2,1)S(1)}, u32[]{:S(2)}, u32[]{:S(2)}) collective-permute-start(bf16[256,1280]{1,0:T(8,128)(2,1)} %copy-done.7), channel_id=1, source_target_pairs={{0,3},{1,0},{2,1},{3,2},{4,7},{5,4},{6,5},{7,6},{8,11},{9,8},{10,9... | collective-permute-start | bytes 1966088 | tf_op jit(solution)/shard_map/ppermute | solution.py:43
